TPU v7x, 512 devices: a whole 4x8x8 slice. The times are simulated.
512 devices in a mesh: dp: 64 (over z_hi, y, core), mp: 8 (over x, z_lo).
Axes of the slice: x: 4, y: 8, z: 8 (z_hi: 4, z_lo: 2; z = z_hi * 2 + z_lo), core: 2. Of those that a mesh axis runs over, the one named last changes fastest.
Arguments:
- tokens: bfloat16 [9216, 4096], P('dp'), may hold values from -6 to 6
- cotangent: bfloat16 [9216, 4096], P('dp'), may hold values from -6 to 6
- gate_blocks: bfloat16 [64, 128, 128], P('dp'), may hold values from -0.5 to 0.5
- up_blocks: bfloat16 [64, 128, 128], P('dp'), may hold values from -0.5 to 0.5
- down_blocks: bfloat16 [64, 128, 128], P('dp'), may hold values from -0.5 to 0.5
- col_block: int32 [64], replicated, may hold values from 0 to 223, as said below
- in_row: int32 [64], replicated, may hold values from 0 to 31, as said below
- out_row: int32 [64], replicated, may hold values from 0 to 31
Outputs:
- input_grad: bfloat16 [9216, 4096], P('dp', 'mp')
- gate_grads: float32 [64, 128, 128], P('dp')
- up_grads: float32 [64, 128, 128], P('dp')
- down_grads: float32 [64, 128, 128], P('dp')
Inputs may be any that keep to these rules, and one draw needn't show every extreme that they name: Flat blocks are ordered by owner: floor(col_block / 28) never falls along the list. Each owner holds 1 to 20 blocks, and some owner holds exactly 20. The pairs (in_row, col_block) are distinct, and so are the pairs (col_block, out_row). `in_row`: gate and up blocks share positions.
All inputs are finite; a program needn't handle non-finite values.
Results may differ from a plain program's by a relative error of at most 0.007.
Values may be sent and summed in bfloat16 or wider, within the bound.
A program may use at most 64 MiB of HBM per device.

v0:
```python
import jax
import jax.numpy as jnp
from jax import lax
from jax.sharding import Mesh
from jax.sharding import PartitionSpec as P

FF = 28672
DP = ("dp_0", "dp_1", "dp_2")


def sent_together(arrays, axis, dim, along):
    both = jnp.concatenate(arrays, axis=along)
    whole, at, finished = (lax.all_gather(both, axis, axis=dim, tiled=True), 0, [])
    for a in arrays:
        finished.append(lax.slice_in_dim(whole, at, at + a.shape[along], axis=along))
        at += a.shape[along]
    return tuple(finished)


def filled_up(lines, size):
    spare = -len(lines) % size
    return jnp.pad(lines, [(0, spare)] + [(0, 0)] * (lines.ndim - 1))


def from_everyone(shard, axis):
    size = lax.axis_size(axis)
    return lax.all_to_all(
        jnp.broadcast_to(shard[None], (size, *shard.shape)), axis, 0, 0, tiled=True
    )


def laid_out(pieces, dim):
    pieces = jnp.moveaxis(pieces, 0, dim)
    lengths = pieces.shape
    return pieces.reshape(*lengths[:dim], lengths[dim] * lengths[dim + 1], *lengths[dim + 2 :])


def gathered_by_axis(shard, axes, dim):
    far, near = axes
    first = from_everyone(shard, far)
    pieces = jnp.swapaxes(from_everyone(first, near), 0, 1)
    return laid_out(pieces.reshape(-1, *shard.shape), dim)


def cut_along(shard, dim, size):
    lengths = shard.shape
    pieces = shard.reshape(*lengths[:dim], size, lengths[dim] // size, *lengths[dim + 1 :])
    return jnp.moveaxis(pieces, dim, 0)


def sent_and_summed(shard, axis, dim):
    size = lax.axis_size(axis)
    pieces = lax.all_to_all(cut_along(shard, dim, size), axis, 0, 0, tiled=True)
    return jnp.sum(pieces, axis=0)


def sum_by_axis(shard, axes, dim):
    far, near = axes
    pieces = cut_along(shard, dim, lax.axis_size(far))
    nearer = sent_and_summed(pieces, near, dim + 1)
    arrived = lax.all_to_all(nearer, far, split_axis=0, concat_axis=0, tiled=True)
    return arrived.sum(axis=0)


def total_of(shard, axes):
    padded = filled_up(shard, lax.axis_size(axes[0]) * lax.axis_size(axes[1]))
    whole = gathered_by_axis(sum_by_axis(padded, axes, 0), axes, 0)
    return lax.slice_in_dim(whole, 0, len(shard)).reshape(shard.shape)


def packed_total(arrays, axis):
    ravelled, at, finished = (jnp.concatenate([a.reshape(-1) for a in arrays]), 0, [])
    subtotal = total_of(ravelled, axis)
    for a in arrays:
        finished.append(subtotal[at : at + a.size].reshape(a.shape))
        at += a.size
    return tuple(finished)


def taken_together(shard, axis):
    return from_everyone(shard, axis).sum(axis=0)


def together(arrays, axis):
    ravelled, at, finished = (jnp.concatenate([a.reshape(-1) for a in arrays]), 0, [])
    subtotal = taken_together(ravelled, axis)
    for a in arrays:
        finished.append(subtotal[at : at + a.size].reshape(a.shape))
        at += a.size
    return tuple(finished)


def sum_at_owner(shard, axis, dim):
    pieces = cut_along(shard, dim, lax.axis_size(axis))
    arrived = lax.all_to_all(pieces, axis, split_axis=0, concat_axis=0, tiled=True)
    return arrived.astype(jnp.float32).sum(axis=0)


def on_device(tokens, cotangent, gate_blocks, up_blocks, down_blocks, col_block, in_row, out_row):
    highest = lax.Precision.HIGHEST
    token_count = tokens.shape[0]
    model_width = tokens.shape[1]
    block_size = gate_blocks.shape[1]
    local_count = gate_blocks.shape[0]
    total_blocks = col_block.shape[0]
    model_count = lax.axis_size("mp")
    model_rank = lax.axis_index("mp")
    data_rank = lax.axis_index(DP)
    row_blocks = model_width // block_size
    owned_cols = FF // (block_size * model_count)
    capacity = min(20, total_blocks - model_count + 1)
    owner_of = col_block // owned_cols
    first_slot = jnp.sum((owner_of < model_rank).astype(jnp.int32))
    owned_count = jnp.sum((owner_of == model_rank).astype(jnp.int32))
    slot_ids = jnp.arange(capacity, dtype=jnp.int32)
    picked = jnp.minimum(first_slot + slot_ids, total_blocks - 1)
    live_slots = slot_ids < owned_count
    every_gate, every_up, every_down = sent_together(
        (gate_blocks, up_blocks, down_blocks), DP, 0, 1
    )

    def select_own(blocks_all):
        taken = jnp.take(blocks_all, picked, axis=0)
        return jnp.where(live_slots[:, None, None], taken, jnp.zeros((), blocks_all.dtype))

    own_gate = select_own(every_gate)
    own_up = select_own(every_up)
    own_down = select_own(every_down)
    columns = jnp.take(col_block, picked)
    rows_in = jnp.take(in_row, picked)
    rows_out = jnp.take(out_row, picked)
    same_column = (
        (columns[:, None] == columns[None, :]) & live_slots[:, None] & live_slots[None, :]
    ).astype(jnp.float32)
    token_in = jnp.take(tokens.reshape(token_count, row_blocks, block_size), rows_in, axis=1)
    cot_in = jnp.take(cotangent.reshape(token_count, row_blocks, block_size), rows_out, axis=1)
    gate_part = jnp.einsum("tkb,kbc->ktc", token_in, own_gate, preferred_element_type=jnp.float32)
    up_part = jnp.einsum("tkb,kbc->ktc", token_in, own_up, preferred_element_type=jnp.float32)
    gate_total = jnp.einsum("jk,ktc->jtc", same_column, gate_part, precision=highest)
    up_total = jnp.einsum("jk,ktc->jtc", same_column, up_part, precision=highest)
    gate_sigmoid = jax.nn.sigmoid(gate_total)
    gate_act = gate_total * gate_sigmoid
    hidden = (gate_act * up_total).astype(jnp.bfloat16)
    down_part = jnp.einsum("tkb,kcb->ktc", cot_in, own_down, preferred_element_type=jnp.float32)
    hidden_grad = jnp.einsum("jk,ktc->jtc", same_column, down_part, precision=highest)
    gate_grad = (
        hidden_grad * up_total * gate_sigmoid * (1.0 + gate_total * (1.0 - gate_sigmoid))
    ).astype(jnp.bfloat16)
    up_grad = (hidden_grad * gate_act).astype(jnp.bfloat16)
    grad_scale = (token_count * lax.axis_size(DP)) ** (-0.5)
    down_term = (
        jnp.einsum("ktc,tkb->kcb", hidden, cot_in, preferred_element_type=jnp.float32) * grad_scale
    )
    gate_term = (
        jnp.einsum("tkb,ktc->kbc", token_in, gate_grad, preferred_element_type=jnp.float32)
        * grad_scale
    )
    up_term = (
        jnp.einsum("tkb,ktc->kbc", token_in, up_grad, preferred_element_type=jnp.float32)
        * grad_scale
    )
    down_sum, gate_sum, up_sum = packed_total(
        (down_term, gate_term, up_term), (("dp_0", "dp_1"), "dp_2")
    )
    flat_ids = data_rank * local_count + jnp.arange(local_count, dtype=jnp.int32)
    is_mine = jnp.take(owner_of, flat_ids) == model_rank
    flat_slot = jnp.clip(flat_ids - first_slot, 0, capacity - 1)

    def place_own(summed):
        return jnp.where(is_mine[:, None, None], jnp.take(summed, flat_slot, axis=0), 0.0)

    gate_flat, up_flat, down_flat = together(
        (place_own(gate_sum), place_own(up_sum), place_own(down_sum)), "mp"
    )
    spread = jnp.einsum("ktc,kbc->ktb", gate_grad, own_gate, preferred_element_type=jnp.float32)
    spread = spread + jnp.einsum(
        "ktc,kbc->ktb", up_grad, own_up, preferred_element_type=jnp.float32
    )
    row_onehot = (rows_in[:, None] == jnp.arange(row_blocks, dtype=jnp.int32)[None, :]).astype(
        jnp.float32
    )
    partial_value = jnp.einsum("kr,ktb->trb", row_onehot, spread, precision=highest).reshape(
        token_count, model_width
    )
    input_grad = sum_at_owner(partial_value.astype(jnp.bfloat16), "mp", 1).astype(jnp.bfloat16)
    return (input_grad, gate_flat, up_flat, down_flat)


def solution(mesh):
    finer = Mesh(mesh.devices.reshape(4, 8, 2, mesh.shape["mp"]), ("dp_0", "dp_1", "dp_2", "mp"))
    placed = (
        P(DP, None),
        P(DP, None),
        P(DP, None, None),
        P(DP, None, None),
        P(DP, None, None),
        P(),
        P(),
        P(),
    )
    return jax.shard_map(
        on_device,
        mesh=finer,
        in_specs=placed,
        out_specs=(P(DP, "mp"), P(DP, None, None), P(DP, None, None), P(DP, None, None)),
        check_vma=False,
    )
```

profile of v0, /device:TPU:1, one launch (start us, length us, event | category | flops | bytes accessed | tf_op | source)
XLA Modules:
  0.0 353.5 jit_solution(17915927918931845261)
XLA Ops:
  7.2 1.5 pad_maximum_fusion.2
  8.8 1.3 fusion.51
  10.8 1.4 gather_fusion
  12.1 1.4 gather_fusion.1
  13.5 0.7 gather_fusion.4
  15.1 1.6 gather_fusion.2
  18.2 0.7 gather_fusion.5
  18.9 1.3 compare_and_fusion.2
  20.2 92.7 %all-gather.2.cloned.1.call-done = bf16[64,384,128]{2,1,0:T(8,128)(2,1)} async-done(((bf16[1,384,128]{2,1,0:T(8,128)(2,1)}), bf16[64,384,128]{2,1,0:T(8,128)(2,1)}) %all-gather.2.cloned.1.call-update) | async-done | bytes 6291472 | tf_op jit(solution)/shard_map/all_gather | solution.py:13
  112.9 7.1 %fusion.57 = (bf16[64,128,128]{2,1,0:T(8,128)(2,1)}, bf16[64,128,128]{2,1,0:T(8,128)(2,1)S(1)}, bf16[64,128,128]{2,1,0:T(8,128)(2,1)}) fusion(bf16[64,384,128]{2,1,0:T(8,128)(2,1)} %all-gather.2.cloned.1.call-done), kind=kLoop, calls=%fused_computation.102 | loop fusion | bytes 12582912 | tf_op jit(solution)/shard_map/slice | solution.py:15
  120.0 3.1 gather_fusion.3
  123.1 1.5 gather_fusion.7
  124.6 1.9 fusion.22
  126.5 1.3 fusion.6
  128.5 2.5 fusion.2
  131.0 3.1 gather_fusion.6
  134.1 1.7 fusion.19
  135.8 1.3 fusion.4
  137.4 0.9 convolution_multiply_fusion.2
  138.3 1.0 multiply_convert_fusion.1
  139.3 0.7 convolution_multiply_fusion
  140.0 0.7 convolution_multiply_fusion.1
  140.7 2.3 pad_maximum_fusion
  143.0 5.6 %reshape_reshape.4 = f32[32,2,15360]{2,1,0:T(2,128)} reshape(f32[983040]{0:T(1024)} %pad_maximum_fusion) | data formatting | bytes 7864320 | tf_op jit(solution)/shard_map/reshape;reshape | solution.py:47
  148.6 3.4 copy.98
  152.0 7.8 %all_to_all.36 = f32[2,32,15360]{2,1,0:T(8,128)} all-to-all(f32[2,32,15360]{2,1,0:T(8,128)S(1)} %copy.98), channel_id=1, replica_groups=mesh['dp_0'=4,'dp_1'=8,'dp_2'=2,'mp'=8] {'dp_2'}, dimensions={0} | all-to-all | bytes 7864320 | tf_op jit(solution)/shard_map/all_to_all | solution.py:53
  159.8 2.6 reduce_sum.60
  162.4 1.3 all_to_all.25
  163.8 53.5 %all_to_all.37 = f32[32,1,15360]{2,1,0:T(1,128)S(1)} all-to-all(f32[32,1,15360]{2,1,0:T(1,128)S(1)} %all_to_all.25), channel_id=1, replica_groups=mesh['dp_0'=4,'dp_1'=8,'dp_2'=2,'mp'=8] {'dp_0','dp_1'}, dimensions={0} | all-to-all | bytes 3932160 | tf_op jit(solution)/shard_map/all_to_all | solution.py:61
  217.3 1.1 reduce_sum.61
  218.4 2.3 broadcast_in_dim.113
  220.7 9.4 %all-to-all-start.3 = ((f32[32,1,15360]{2,1,0:T(1,128)}), f32[32,1,15360]{2,1,0:T(1,128)S(1)}, u32[]{:S(2)}, u32[]{:S(2)}) async-start(f32[32,1,15360]{2,1,0:T(1,128)} %broadcast_in_dim.113), calls=%async_computation.3 | async-start | bytes 3932160 | tf_op jit(solution)/shard_map/all_to_all | solution.py:27
  230.2 2.0 fusion.56
  232.9 1.6 fusion.12
  234.5 1.6 convert_element_type.35
  236.0 2.7 copy.137
  238.7 44.1 %all-to-all-done.3 = f32[32,1,15360]{2,1,0:T(1,128)S(1)} async-done(((f32[32,1,15360]{2,1,0:T(1,128)}), f32[32,1,15360]{2,1,0:T(1,128)S(1)}, u32[]{:S(2)}, u32[]{:S(2)}) %all-to-all-start.3) | async-done | bytes 1966112 | tf_op jit(solution)/shard_map/all_to_all | solution.py:27
  283.5 10.8 %all_to_all.38 = f32[2,32,15360]{2,1,0:T(8,128)} all-to-all(f32[2,32,15360]{2,1,0:T(8,128)S(1)} %broadcast_in_dim.115), channel_id=1, replica_groups=mesh['dp_0'=4,'dp_1'=8,'dp_2'=2,'mp'=8] {'dp_2'}, dimensions={0} | all-to-all | bytes 7864320 | tf_op jit(solution)/shard_map/all_to_all | solution.py:27
  294.3 5.4 %all-to-all-start = ((bf16[8,144,512]{2,1,0:T(8,128)(2,1)}), bf16[8,144,512]{2,1,0:T(8,128)(2,1)S(1)}, u32[]{:S(2)}, u32[]{:S(2)}) async-start(bf16[8,144,512]{2,1,0:T(8,128)(2,1)} %bitcast.73), calls=%async_computation | async-start | bytes 2359296 | tf_op jit(solution)/shard_map/all_to_all | solution.py:95
  301.7 7.0 %copy.99 = f32[32,2,15360]{2,1,0:T(2,128)} copy(f32[32,2,15360]{2,0,1:T(8,128)} %bitcast.74) | data formatting | bytes 7864320 | tf_op jit(solution)/shard_map/transpose | solution.py:41
  308.8 6.1 %slice.65 = f32[60,128,128]{2,1,0:T(8,128)} reshape(f32[32,2,15360]{2,1,0:T(2,128)} %copy.99) | data formatting | bytes 7864320 | tf_op jit(solution)/shard_map/slice | solution.py:75
  314.8 2.5 fusion.58
  317.5 2.0 broadcast_in_dim.117
  319.5 5.1 %all-to-all-start.5 = ((f32[8,1,49152]{2,1,0:T(1,128)}), f32[8,1,49152]{2,1,0:T(1,128)S(1)}, u32[]{:S(2)}, u32[]{:S(2)}) async-start(f32[8,1,49152]{2,1,0:T(1,128)} %broadcast_in_dim.117), calls=%async_computation.5 | async-start | bytes 3145728 | tf_op jit(solution)/shard_map/all_to_all | solution.py:27
  324.6 2.2 reduce_sum.59
  326.8 17.9 %all-to-all-done.5 = f32[8,1,49152]{2,1,0:T(1,128)S(1)} async-done(((f32[8,1,49152]{2,1,0:T(1,128)}), f32[8,1,49152]{2,1,0:T(1,128)S(1)}, u32[]{:S(2)}, u32[]{:S(2)}) %all-to-all-start.5) | async-done | bytes 1572896 | tf_op jit(solution)/shard_map/all_to_all | solution.py:27
  344.8 1.1 reduce_sum.62
  345.9 0.7 slice_bitcast_fusion
  (45 shorter events, 6.0 us)
Async XLA Ops:
  7.2 7.7 %copy-start = (bf16[144,4096]{1,0:T(8,128)(2,1)S(1)}, bf16[144,4096]{1,0:T(8,128)(2,1)}, u32[]{:S(2)}) copy-start(bf16[144,4096]{1,0:T(8,128)(2,1)} %param.17) | copy-start | bytes 3538948
  7.2 6.3 %copy-start.2 = (s32[64]{0:T(128)S(1)}, s32[64]{0:T(128)}, u32[]{:S(2)}) copy-start(s32[64]{0:T(128)} %param.22) | copy-start | bytes 772
  7.2 105.7 %all-gather.2.cloned.1.call-start = ((), (), s32[]{:S(2)}) async-start(), calls=%async_computation.6 | async-start | bytes 6389760 | tf_op jit(solution)/shard_map/all_gather | solution.py:13
  15.1 2.9 copy-start.10
  126.5 1.3 copy-start.9
  135.8 1.5 copy-start.3
  135.8 1.6 copy-start.11
  139.3 1.4 copy-start.4
  139.3 1.4 copy-start.6
  220.7 62.1 %all-to-all-start.3 = ((f32[32,1,15360]{2,1,0:T(1,128)}), f32[32,1,15360]{2,1,0:T(1,128)S(1)}, u32[]{:S(2)}, u32[]{:S(2)}) async-start(f32[32,1,15360]{2,1,0:T(1,128)} %broadcast_in_dim.113), calls=%async_computation.3 | async-start | bytes 3932160 | tf_op jit(solution)/shard_map/all_to_all | solution.py:27
  230.1 2.1 copy-start.5
  230.1 2.1 copy-start.8
  294.3 23.2 %all-to-all-start = ((bf16[8,144,512]{2,1,0:T(8,128)(2,1)}), bf16[8,144,512]{2,1,0:T(8,128)(2,1)S(1)}, u32[]{:S(2)}, u32[]{:S(2)}) async-start(bf16[8,144,512]{2,1,0:T(8,128)(2,1)} %bitcast.73), calls=%async_computation | async-start | bytes 2359296 | tf_op jit(solution)/shard_map/all_to_all | solution.py:95
  317.5 2.0 copy-start.7
  319.5 25.3 %all-to-all-start.5 = ((f32[8,1,49152]{2,1,0:T(1,128)}), f32[8,1,49152]{2,1,0:T(1,128)S(1)}, u32[]{:S(2)}, u32[]{:S(2)}) async-start(f32[8,1,49152]{2,1,0:T(1,128)} %broadcast_in_dim.117), calls=%async_computation.5 | async-start | bytes 3145728 | tf_op jit(solution)/shard_map/all_to_all | solution.py:27
  324.6 22.0 %copy-start.1 = (bf16[144,4096]{1,0:T(8,128)(2,1)S(1)}, bf16[144,4096]{1,0:T(8,128)(2,1)}, u32[]{:S(2)}) copy-start(bf16[144,4096]{1,0:T(8,128)(2,1)} %param.17) | copy-start | bytes 3538948
Sparse Core Ops, SparseCore 0:
  11.9 100.9 all-gather.1
where the time goes:
time: 356 us; the launch traced here: 353 us
  waiting for transfers between devices  155 us (44%)
  blocking collectives  72.2 us (20%)
  local copies, waits for them, and re-layouts  57.6 us (16%)
  starting transfers between devices  20 us (6%)
  other arithmetic  17.2 us (5%)
  matrix products  15.9 us (4%)
  between operations  15.8 us (4%)
    all_gather x1, waiting for transfers between devices, sent_together(): lax.all_gather(both, axis, axis=dim, tiled=True)  92.7 us
    all_to_all x2, waiting for transfers between devices, from_everyone(): lax.all_to_all(jnp.broadcast_to(shard[None], (size, *shard.shape)), axis,...  62.1 us
    all_to_all x1, blocking collectives, sum_by_axis(): lax.all_to_all(nearer, far, split_axis=0, concat_axis=0, tiled=True)  53.5 us
    all_to_all x2, starting transfers between devices, from_everyone(): lax.all_to_all(jnp.broadcast_to(shard[None], (size, *shard.shape)), axis,...  14.5 us
    all_to_all x1, blocking collectives, from_everyone(): lax.all_to_all(jnp.broadcast_to(shard[None], (size, *shard.shape)), axis,...  10.8 us
    slice x2, local copies, waits for them, and re-layouts, packed_total(): finished.append(subtotal[at:at + a.size].reshape(a.shape))  8.6 us
    all_to_all x1, blocking collectives, sent_and_summed(): pieces = lax.all_to_all(cut_along(shard, dim, size), axis, 0, 0, tiled=True)  7.83 us
    gather x3, local copies, waits for them, and re-layouts, select_own(): taken = jnp.take(blocks_all, picked, axis=0)  7.69 us
  transfers between devices with their start and end apart: 4, of which 3 were waited for; matrix products, arithmetic and copies ran while one was open for 11% of the time, Pallas kernels for 0%

commit v1 on v0

v1 whole, which is shorter than its diff:
```python
import jax
import jax.numpy as jnp
from jax import lax
from jax.experimental import pallas as pl
from jax.experimental.pallas import tpu as pltpu
from jax.sharding import Mesh
from jax.sharding import PartitionSpec as P

AXES = ("zh", "y", "c", "x", "zl")
SIZE = {"zh": 4, "y": 8, "c": 2, "x": 4, "zl": 2}
BLK = 128
TOK = 144
D = 4096
NB = 64
SUB = 16
MESH_ID = pl.DeviceIdType.MESH
F32, BF16 = jnp.float32, jnp.bfloat16
Y_OFF = (4, 3, 5, 2, 6, 1, 7)
Z_OFF = (2, 1, 3)
MP_OFF = ((2, 0), (2, 1), (1, 0), (3, 0), (1, 1), (3, 1), (0, 1))


def at(axis, offset):
    return lax.rem(lax.axis_index(axis) + (SIZE[axis] + offset), SIZE[axis])


def sibling():
    return {"c": 1 - lax.axis_index("c")}


def mp_peer(off):
    return {"x": at("x", off[0]), "zl": at("zl", off[1])}


def enter(devices):
    barrier = pltpu.get_barrier_semaphore()
    for d in devices:
        pl.semaphore_signal(barrier, inc=1, device_id=d, device_id_type=MESH_ID)
    pl.semaphore_wait(barrier, len(devices))


def send(src, dst, s, r, device):
    copy = pltpu.make_async_remote_copy(
        src_ref=src, dst_ref=dst, send_sem=s, recv_sem=r, device_id=device, device_id_type=MESH_ID
    )
    copy.start()
    return copy


def gather_kernel(gate, up, down, a_out, b_out, own_a, own_b, tg, tu, s_sem, r_sem, s_sib, r_sib):
    c, z, y = lax.axis_index("c"), lax.axis_index("zh"), lax.axis_index("y")
    rows = pl.ds((lax.axis_index("x") * 2 + lax.axis_index("zl")) * SUB, SUB)
    tg[...] = gate[0].astype(F32).T
    tu[...] = up[0].astype(F32).T
    own_a[0:SUB] = tg[rows].astype(BF16)
    own_a[SUB:] = tu[rows].astype(BF16)
    own_b[...] = down[0, rows]
    a_out[c, y, z] = own_a[...]
    b_out[c, z, y] = own_b[...]
    enter([{"zh": at("zh", o)} for o in Z_OFF] + [{"y": at("y", o)} for o in Y_OFF] + [sibling()])
    a1 = [
        send(own_a, a_out.at[c, y, z], s_sem.at[o], r_sem.at[o], {"zh": at("zh", o)})
        for o in Z_OFF
    ]
    b1 = [
        send(own_b, b_out.at[c, z, y], s_sem.at[8 + o], r_sem.at[8 + o], {"y": at("y", o)})
        for o in Y_OFF
    ]
    for copy in a1:
        copy.wait_recv()
    a2 = [
        send(a_out.at[c, y], a_out.at[c, y], s_sem.at[16 + o], r_sem.at[16 + o], {"y": at("y", o)})
        for o in Y_OFF
    ]
    for copy in b1:
        copy.wait_recv()
    b2 = [
        send(b_out.at[c, z], b_out.at[c, z], s_sem.at[4 + o], r_sem.at[4 + o], {"zh": at("zh", o)})
        for o in Z_OFF
    ]
    shared = []

    def share(ref, index, slot):
        part = ref.at[c, index]
        shared.append(send(part, part, s_sib.at[slot], r_sib.at[slot], sibling()))

    share(a_out, y, 0)
    share(b_out, z, 8)
    for o, copy in list(zip(Y_OFF, a2))[::-1][:4]:
        copy.wait_recv()
        share(a_out, at("y", -o), o)
    for o, copy in list(zip(Z_OFF, b2))[::-1]:
        copy.wait_recv()
        share(b_out, at("zh", -o), 8 + o)
    for o, copy in list(zip(Y_OFF, a2))[:3][::-1]:
        copy.wait_recv()
        share(a_out, at("y", -o), o)
    for copy in shared:
        copy.wait()
    for copy in a1 + b1 + a2 + b2:
        copy.wait_send()


def gathered(gate, up, down):
    vmem = pl.BlockSpec(memory_space=pltpu.VMEM)
    return pl.pallas_call(
        gather_kernel,
        name="gather_blocks",
        out_shape=(
            jax.ShapeDtypeStruct((2, 8, 4, 2 * SUB, BLK), BF16),
            jax.ShapeDtypeStruct((2, 4, 8, SUB, BLK), BF16),
        ),
        in_specs=[vmem] * 3,
        out_specs=(vmem, vmem),
        scratch_shapes=[
            pltpu.VMEM((2 * SUB, BLK), BF16),
            pltpu.VMEM((SUB, BLK), BF16),
            pltpu.VMEM((BLK, BLK), F32),
            pltpu.VMEM((BLK, BLK), F32),
            pltpu.SemaphoreType.DMA((24,)),
            pltpu.SemaphoreType.DMA((24,)),
            pltpu.SemaphoreType.DMA((12,)),
            pltpu.SemaphoreType.DMA((12,)),
        ],
        compiler_params=pltpu.CompilerParams(
            collective_id=0, has_side_effects=True, vmem_limit_bytes=32 << 20
        ),
    )(gate, up, down)


def flat_of(p):
    return (p % 4) * 16 + ((p // 4) % 8) * 2 + p // 32


def place_of(k):
    return (k % 2) * 32 + ((k // 2) % 8) * 4 + k // 16


def dot_nt(a, b):
    return lax.dot_general(a, b, (((1,), (1,)), ((), ())), preferred_element_type=F32)


def dot(a, b):
    return jnp.dot(a, b, preferred_element_type=F32)


def compute_kernel(slot, in_row, out_row, tok, cot, a, b, part, wa, wb, w, dn, g_s, u_s, h_s, acc):
    def columns(ref, row):
        return ref[:, pl.ds(pl.multiple_of(row * BLK, BLK), BLK)]

    w[...] = jnp.zeros_like(w)
    dn[...] = jnp.zeros_like(dn)
    acc[...] = jnp.zeros_like(acc)

    @pl.loop(0, 8)
    def _(t):
        xs, ys = [], []
        for i in range(8):
            core, yy, zz = t // 4, (t % 4) * 2 + i // 4, i % 4
            k = zz * 16 + yy * 2 + core
            lanes = slice(i * BLK, (i + 1) * BLK)
            w[t, i * SUB : (i + 1) * SUB, lanes] = a[core, yy, zz, 0:SUB]
            w[t, BLK + i * SUB : BLK + (i + 1) * SUB, lanes] = a[core, yy, zz, SUB:]
            dn[t, i * SUB : (i + 1) * SUB, lanes] = b[core, zz, yy]
            xs.append(columns(tok, in_row[k]))
            ys.append(columns(cot, out_row[k]))
        gu = dot_nt(jnp.concatenate(xs, axis=1), w[t])
        g_s[t] = gu[:, :BLK]
        u_s[t] = gu[:, BLK:]
        h_s[t] = dot_nt(jnp.concatenate(ys, axis=1), dn[t])

    group = lax.broadcasted_iota(jnp.int32, (TOK, BLK), 1) // SUB

    @pl.loop(0, NB)
    def _(p):
        k = flat_of(p)

        @pl.when(slot[k] != k)
        def _():
            q = place_of(slot[k])
            shift = lax.rem((q - p) * SUB + 16 * BLK, BLK)
            for s in (g_s, u_s, h_s):
                moved = pltpu.roll(s[p // 8], shift, axis=1)
                s[q // 8] += jnp.where(group == q % 8, moved, 0.0)

    @pl.loop(0, NB)
    def _(p):
        k = flat_of(p)

        @pl.when(slot[k] != k)
        def _():
            q = place_of(slot[k])
            shift = lax.rem((p - q) * SUB + 16 * BLK, BLK)
            for s in (g_s, u_s, h_s):
                moved = pltpu.roll(s[q // 8], shift, axis=1)
                s[p // 8] = jnp.where(group == p % 8, moved, s[p // 8])

    @pl.loop(0, 8)
    def _(t):
        gate, up, hg = g_s[t], u_s[t], h_s[t]
        sig = jax.nn.sigmoid(gate)
        act = gate * sig
        hid = (act * up).T.astype(BF16)
        gg = hg * up * sig * (1.0 + gate * (1.0 - sig))
        ug = hg * act
        ggt, ugt = gg.T.astype(BF16), ug.T.astype(BF16)
        spread = dot(jnp.concatenate([gg.astype(BF16), ug.astype(BF16)], axis=1), w[t])
        for i in range(8):
            core, yy, zz = t // 4, (t % 4) * 2 + i // 4, i % 4
            k = zz * 16 + yy * 2 + core
            acc[in_row[k]] += spread[:, i * BLK : (i + 1) * BLK]
        for j in range(4):
            rows = slice(32 * j, 32 * j + 32)
            idx = []
            for i in (2 * j, 2 * j + 1):
                idx.append((t // 4, (t % 4) * 2 + i // 4, i % 4))
            ks = [zz * 16 + yy * 2 + core for core, yy, zz in idx]
            left = jnp.concatenate([ggt[rows], ugt[rows]], axis=0)
            r = dot(left, jnp.concatenate([columns(tok, in_row[k]) for k in ks], axis=1))
            d = dot(hid[rows], jnp.concatenate([columns(cot, out_row[k]) for k in ks], axis=1))
            for n, (core, yy, zz) in enumerate(idx):
                lanes = slice(n * BLK, (n + 1) * BLK)
                wa[core, yy, zz, 0:SUB] = r[n * SUB : (n + 1) * SUB, lanes]
                wa[core, yy, zz, SUB:] = r[32 + n * SUB : 32 + (n + 1) * SUB, lanes]
                wb[core, zz, yy] = d[n * SUB : (n + 1) * SUB, lanes]

    for m in range(8):
        for j in range(4):
            part[m, :, j * BLK : (j + 1) * BLK] = acc[4 * m + j].astype(BF16)


def computed(slot, in_row, out_row, tok, cot, a, b):
    vmem = pl.BlockSpec(memory_space=pltpu.VMEM)
    smem = pl.BlockSpec(memory_space=pltpu.SMEM)
    return pl.pallas_call(
        compute_kernel,
        name="block_grads",
        out_shape=(
            jax.ShapeDtypeStruct((8, TOK, 512), BF16),
            jax.ShapeDtypeStruct((2, 8, 4, 2 * SUB, BLK), F32),
            jax.ShapeDtypeStruct((2, 4, 8, SUB, BLK), F32),
        ),
        in_specs=[smem] * 3 + [vmem] * 4,
        out_specs=(vmem,) * 3,
        scratch_shapes=[
            pltpu.VMEM((8, 256, 1024), BF16),
            pltpu.VMEM((8, 128, 1024), BF16),
            pltpu.VMEM((8, TOK, BLK), F32),
            pltpu.VMEM((8, TOK, BLK), F32),
            pltpu.VMEM((8, TOK, BLK), F32),
            pltpu.VMEM((32, TOK, BLK), F32),
        ],
        compiler_params=pltpu.CompilerParams(vmem_limit_bytes=48 << 20),
    )(slot, in_row, out_row, tok, cot, a, b)


def reduce_kernel(
    part, wa, wb, ig_out, g_out, u_out, d_out,
    ig_in, sib_a, sib_b, sum_a, sum_b, in_a1, in_b1, sum_a2, sum_b2, in_a2, in_b2, fin,
    s_sem, r_sem, s_mp, r_mp, s_fin, r_fin,
):
    c, z, y = lax.axis_index("c"), lax.axis_index("zh"), lax.axis_index("y")
    x, zl = lax.axis_index("x"), lax.axis_index("zl")
    m = x * 2 + zl
    enter(
        [{"zh": at("zh", o)} for o in Z_OFF]
        + [{"y": at("y", o)} for o in Y_OFF]
        + [sibling()]
        + [mp_peer(o) for o in MP_OFF]
    )
    o = 1 - c
    sib = [
        send(wa.at[o], sib_a, s_sem.at[0], r_sem.at[0], sibling()),
        send(wb.at[o], sib_b, s_sem.at[8], r_sem.at[8], sibling()),
    ]
    exch = []
    for i, off in enumerate(MP_OFF):
        peer = mp_peer(off)
        exch.append(
            send(part.at[peer["x"] * 2 + peer["zl"]], ig_in.at[i], s_mp.at[i], r_mp.at[i], peer)
        )
    sib[0].wait_recv()
    sum_a[...] = (wa[c] + sib_a[...]).astype(BF16)
    a1 = []
    for off in Y_OFF:
        q = at("y", off)
        a1.append(
            send(sum_a.at[q], in_a1.at[off], s_sem.at[16 + off], r_sem.at[16 + off], {"y": q})
        )
    sib[1].wait_recv()
    sum_b[...] = (wb[c] + sib_b[...]).astype(BF16)
    b1 = []
    for off in Z_OFF:
        q = at("zh", off)
        b1.append(
            send(sum_b.at[q], in_b1.at[off], s_sem.at[4 + off], r_sem.at[4 + off], {"zh": q})
        )
    total = sum_b[z].astype(F32)
    for off, copy in zip(Z_OFF, b1):
        copy.wait_recv()
        total += in_b1[off].astype(F32)
    sum_b2[...] = total.astype(BF16)
    b2 = []
    for off in Y_OFF:
        q = at("y", off)
        b2.append(
            send(sum_b2.at[q], in_b2.at[off], s_sem.at[8 + off], r_sem.at[8 + off], {"y": q})
        )
    total = sum_a[y].astype(F32)
    for off, copy in zip(Y_OFF, a1):
        copy.wait_recv()
        total += in_a1[off].astype(F32)
    sum_a2[...] = total.astype(BF16)
    a2 = []
    for off in Z_OFF:
        q = at("zh", off)
        a2.append(send(sum_a2.at[q], in_a2.at[off], s_sem.at[off], r_sem.at[off], {"zh": q}))
    total = sum_b2[y].astype(F32)
    for off, copy in zip(Y_OFF, b2):
        copy.wait_recv()
        total += in_b2[off].astype(F32)
    fin[m, 2 * SUB :] = total
    total = sum_a2[z].astype(F32)
    for off, copy in zip(Z_OFF, a2):
        copy.wait_recv()
        total += in_a2[off].astype(F32)
    fin[m, 0 : 2 * SUB] = total
    last = [
        send(fin.at[m], fin.at[m], s_fin.at[i], r_fin.at[i], mp_peer(off))
        for i, off in enumerate(MP_OFF)
    ]
    total = part[m].astype(F32)
    for i, copy in enumerate(exch):
        copy.wait_recv()
        total += ig_in[i].astype(F32)
    ig_out[...] = total.astype(BF16)
    for copy in last:
        copy.wait_recv()
    scale = 9216**-0.5
    g_out[0] = fin[:, 0:SUB].reshape(BLK, BLK).T * scale
    u_out[0] = fin[:, SUB : 2 * SUB].reshape(BLK, BLK).T * scale
    d_out[0] = fin[:, 2 * SUB :].reshape(BLK, BLK) * scale
    for copy in sib + exch + a1 + b1 + a2 + b2 + last:
        copy.wait_send()


def reduced(part, wa, wb):
    vmem = pl.BlockSpec(memory_space=pltpu.VMEM)
    grad = jax.ShapeDtypeStruct((1, BLK, BLK), F32)
    return pl.pallas_call(
        reduce_kernel,
        name="sum_grads",
        out_shape=(jax.ShapeDtypeStruct((TOK, 512), BF16), grad, grad, grad),
        in_specs=[vmem] * 3,
        out_specs=(vmem,) * 4,
        scratch_shapes=[
            pltpu.VMEM((7, TOK, 512), BF16),
            pltpu.VMEM((8, 4, 2 * SUB, BLK), F32),
            pltpu.VMEM((4, 8, SUB, BLK), F32),
            pltpu.VMEM((8, 4, 2 * SUB, BLK), BF16),
            pltpu.VMEM((4, 8, SUB, BLK), BF16),
            pltpu.VMEM((8, 4, 2 * SUB, BLK), BF16),
            pltpu.VMEM((4, 8, SUB, BLK), BF16),
            pltpu.VMEM((4, 2 * SUB, BLK), BF16),
            pltpu.VMEM((8, SUB, BLK), BF16),
            pltpu.VMEM((4, 2 * SUB, BLK), BF16),
            pltpu.VMEM((8, SUB, BLK), BF16),
            pltpu.VMEM((8, 3 * SUB, BLK), F32),
            pltpu.SemaphoreType.DMA((24,)),
            pltpu.SemaphoreType.DMA((24,)),
            pltpu.SemaphoreType.DMA((7,)),
            pltpu.SemaphoreType.DMA((7,)),
            pltpu.SemaphoreType.DMA((7,)),
            pltpu.SemaphoreType.DMA((7,)),
        ],
        compiler_params=pltpu.CompilerParams(
            collective_id=1, has_side_effects=True, vmem_limit_bytes=32 << 20
        ),
    )(part, wa, wb)


def on_device(tokens, cotangent, gate, up, down, col_block, in_row, out_row):
    slot = jnp.argmax(col_block[:, None] == col_block[None, :], axis=1).astype(jnp.int32)
    a, b = gathered(gate, up, down)
    part, wa, wb = computed(slot, in_row, out_row, tokens, cotangent, a, b)
    return reduced(part, wa, wb)


def solution(mesh):
    fine = Mesh(mesh.devices.reshape(4, 8, 2, 4, 2), AXES)
    dp, mp = ("zh", "y", "c"), ("x", "zl")
    return jax.shard_map(
        on_device,
        mesh=fine,
        in_specs=(P(dp, None), P(dp, None), P(dp), P(dp), P(dp), P(), P(), P()),
        out_specs=(P(dp, mp), P(dp), P(dp), P(dp)),
        check_vma=False,
    )
```

time: 356 us -> 82.9 us (0.23)
  the two profiles are of different devices: /device:TPU:1 before, /device:TPU:8 now
where the time goes in v1:
time: 82.9 us; the launch traced here: 82.4 us
  Pallas kernels  71.7 us (86%)
  local copies, waits for them, and re-layouts  8.67 us (10%)
  other arithmetic  1.43 us (2%)
    pallas_call x1, Pallas kernels, reduced(): pl.pallas_call(reduce_kernel, name='sum_grads', out_shape=(jax.ShapeDtype...  34.4 us
    pallas_call x1, Pallas kernels, gathered(): pl.pallas_call(gather_kernel, name='gather_blocks', out_shape=(jax.ShapeD...  25.3 us
    pallas_call x1, Pallas kernels, computed(): pl.pallas_call(compute_kernel, name='block_grads', out_shape=(jax.ShapeDt...  12 us
    unnamed x18, local copies, waits for them, and re-layouts  8.67 us

profile of v1, /device:TPU:8, one launch (start us, length us, event | category | flops | bytes accessed | tf_op | source)
XLA Modules:
  0.0 82.4 jit_solution(3261493169129801339)
XLA Ops:
  0.6 1.4 %iota_reduce_fusion = (pred[64]{0:T(512)(128)(4,1)}, s32[64]{0:T(128)S(1)}) fusion(s32[64]{0:T(128)} %param.13), kind=kLoop, calls=%fused_computation | loop fusion | flops 32320 | bytes 576 | tf_op jit(solution)/shard_map/on_device/reduce | solution.py:383
  2.1 0.0 copy-start.2
  2.1 0.8 copy-done.2
  2.8 0.0 copy-start.3
  2.8 0.8 copy-done.3
  3.6 0.0 copy-start.4
  3.6 0.8 copy-done.4
  4.3 25.3 %gather_blocks.1 = (bf16[2,8,4,32,128]{4,3,2,1,0:T(8,128)(2,1)S(1)}, bf16[2,4,8,16,128]{4,3,2,1,0:T(8,128)(2,1)S(1)}) custom-call(bf16[1,128,128]{2,1,0:T(8,128)(2,1)S(1)} %copy-done.2, bf16[1,128,128]{2,1,0:T(8,128)(2,1)S(1)} %copy-done.3, bf16[1,128,128]{2,1,0:T(8,128)(2,1)S(1)} %copy-done.4), custom_call_target="tpu_custom_call" | custom-call | tf_op jit(solution)/shard_map/gather_blocks/pallas_call | solution.py:106
  29.6 0.0 copy-start
  29.6 1.3 %copy-done = bf16[144,4096]{1,0:T(8,128)(2,1)S(1)} copy-done((bf16[144,4096]{1,0:T(8,128)(2,1)S(1)}, bf16[144,4096]{1,0:T(8,128)(2,1)}, u32[]{:S(2)}) %copy-start) | copy-done | bytes 1179672
  30.9 0.0 copy-start.1
  30.9 1.3 %copy-done.1 = bf16[144,4096]{1,0:T(8,128)(2,1)S(1)} copy-done((bf16[144,4096]{1,0:T(8,128)(2,1)S(1)}, bf16[144,4096]{1,0:T(8,128)(2,1)}, u32[]{:S(2)}) %copy-start.1) | copy-done | bytes 1179672
  32.2 0.0 copy-start.5
  32.2 0.7 copy-done.5
  32.8 0.0 copy-start.6
  32.8 0.7 copy-done.6
  33.5 12.0 %block_grads.1 = (bf16[8,144,512]{2,1,0:T(8,128)(2,1)S(1)}, f32[2,8,4,32,128]{4,3,2,1,0:T(8,128)S(1)}, f32[2,4,8,16,128]{4,3,2,1,0:T(8,128)S(1)}) custom-call(s32[64]{0:T(128)S(1)} %get-tuple-element.10.slot, s32[64]{0:T(128)S(1)} %copy-done.5, s32[64]{0:T(128)S(1)} %copy-done.6, bf16[144,4096]{1,0:T(8,128)(2,1)S(1)} %copy-done, ...), custom_call_target="tpu_custom_call" | custom-call | tf_op jit(solution)/shard_map/block_grads/pallas_call | solution.py:235
  45.5 34.4 %sum_grads.1 = (bf16[144,512]{1,0:T(8,128)(2,1)S(1)}, f32[1,128,128]{2,1,0:T(8,128)S(1)}, f32[1,128,128]{2,1,0:T(8,128)S(1)}, f32[1,128,128]{2,1,0:T(8,128)S(1)}) custom-call(bf16[8,144,512]{2,1,0:T(8,128)(2,1)S(1)} %get-tuple-element.13.part, f32[2,8,4,32,128]{4,3,2,1,0:T(8,128)S(1)} %get-tuple-element.14.wa, f32[2,4,8,16,128]{4,3,2,1,0:T(8,128)S(1)} %get-tuple-element.15.wb), custom_call_target="tpu_custom_call" | custom-call | tf_op jit(solution)/shard_map/sum_grads/pallas_call | solution.py:350
  79.9 0.7 copy.16
  80.5 0.6 copy.17
  81.2 0.6 copy.18
  81.8 0.6 copy.19
Async XLA Ops:
  2.1 0.8 copy-start.2
  2.8 0.8 copy-start.3
  3.6 0.8 copy-start.4
  29.6 1.3 %copy-start = (bf16[144,4096]{1,0:T(8,128)(2,1)S(1)}, bf16[144,4096]{1,0:T(8,128)(2,1)}, u32[]{:S(2)}) copy-start(bf16[144,4096]{1,0:T(8,128)(2,1)} %tok.1) | copy-start | bytes 3538948
  30.9 1.3 %copy-start.1 = (bf16[144,4096]{1,0:T(8,128)(2,1)S(1)}, bf16[144,4096]{1,0:T(8,128)(2,1)}, u32[]{:S(2)}) copy-start(bf16[144,4096]{1,0:T(8,128)(2,1)} %cot.1) | copy-start | bytes 3538948
  32.2 0.7 copy-start.5
  32.8 0.7 copy-start.6

commit v2 on v1

v2 whole, which is shorter than its diff:
```python
import jax
import jax.numpy as jnp
from jax import lax
from jax.experimental import pallas as pl
from jax.experimental.pallas import tpu as pltpu
from jax.sharding import Mesh
from jax.sharding import PartitionSpec as P

AXES = ("zh", "y", "c", "x", "zl")
SIZE = {"zh": 4, "y": 8, "c": 2, "x": 4, "zl": 2}
BLK = 128
TOK = 144
D = 4096
NB = 64
SUB = 16
MESH_ID = pl.DeviceIdType.MESH
F32, BF16 = jnp.float32, jnp.bfloat16
Y_OFF = (4, 3, 5, 2, 6, 1, 7)
Z_OFF = (2, 1, 3)
X_OFF = (2, 1, 3)
MP_OFF = ((2, 0), (2, 1), (1, 0), (3, 0), (1, 1), (3, 1), (0, 1))


def at(axis, offset):
    return lax.rem(lax.axis_index(axis) + (SIZE[axis] + offset), SIZE[axis])


def sibling():
    return {"c": 1 - lax.axis_index("c")}


def mp_peer(off):
    return {"x": at("x", off[0]), "zl": at("zl", off[1])}


def enter(devices):
    barrier = pltpu.get_barrier_semaphore()
    for d in devices:
        pl.semaphore_signal(barrier, inc=1, device_id=d, device_id_type=MESH_ID)
    pl.semaphore_wait(barrier, len(devices))


def send(src, dst, s, r, device):
    copy = pltpu.make_async_remote_copy(
        src_ref=src, dst_ref=dst, send_sem=s, recv_sem=r, device_id=device, device_id_type=MESH_ID
    )
    copy.start()
    return copy


def gather_kernel(
    gate, up, down, tok, cot, col, in_row, out_row,
    w, dn, tok_v, cot_v, meta,
    a_in, b_in, own_a, own_b, raw, lists, s_sem, r_sem, s_sib, r_sib, local,
):
    c, z, y = lax.axis_index("c"), lax.axis_index("zh"), lax.axis_index("y")
    rows = pl.ds((lax.axis_index("x") * 2 + lax.axis_index("zl")) * SUB, SUB)
    partners = (
        [{"zh": at("zh", o)} for o in Z_OFF] + [{"y": at("y", o)} for o in Y_OFF] + [sibling()]
    )
    barrier = pltpu.get_barrier_semaphore()
    for d in partners:
        pl.semaphore_signal(barrier, inc=1, device_id=d, device_id_type=MESH_ID)
    meta[...] = jnp.zeros_like(meta)
    loads = [
        pltpu.make_async_copy(src, dst, local.at[i])
        for i, (src, dst) in enumerate(
            (
                (gate.at[0], raw.at[0]),
                (up.at[0], raw.at[1]),
                (down.at[0, rows], own_b),
                (col, lists.at[0]),
                (in_row, lists.at[1]),
                (out_row, lists.at[2]),
                (tok, tok_v),
                (cot, cot_v),
            )
        )
    ]
    for copy in loads:
        copy.start()
    for i in range(2):
        loads[i].wait()
    turned = [raw[i].astype(F32).T.astype(BF16) for i in range(2)]
    for i in range(2):
        raw[i] = turned[i]
    for i in range(2):
        own_a[i * SUB : (i + 1) * SUB] = raw[i, rows]
    loads[2].wait()
    a_in[c, y, z] = own_a[...]
    b_in[c, z, y] = own_b[...]
    pl.semaphore_wait(barrier, len(partners))
    a1 = [
        send(own_a, a_in.at[c, y, z], s_sem.at[o], r_sem.at[o], {"zh": at("zh", o)})
        for o in Z_OFF
    ]
    b1 = [
        send(own_b, b_in.at[c, z, y], s_sem.at[8 + o], r_sem.at[8 + o], {"y": at("y", o)})
        for o in Y_OFF
    ]
    for copy in a1:
        copy.wait_recv()
    a2 = [
        send(a_in.at[c, y], a_in.at[c, y], s_sem.at[16 + o], r_sem.at[16 + o], {"y": at("y", o)})
        for o in Y_OFF
    ]
    for copy in b1:
        copy.wait_recv()
    b2 = [
        send(b_in.at[c, z], b_in.at[c, z], s_sem.at[4 + o], r_sem.at[4 + o], {"zh": at("zh", o)})
        for o in Z_OFF
    ]
    shared = []

    def share(ref, index, slot):
        part = ref.at[c, index]
        shared.append(send(part, part, s_sib.at[slot], r_sib.at[slot], sibling()))

    share(a_in, y, 0)
    share(b_in, z, 8)

    @pl.loop(0, 8)
    def _(t):
        w[t] = jnp.zeros_like(w[t])
        dn[t] = jnp.zeros_like(dn[t])

    for copy in loads[3:]:
        copy.wait()
    meta[0:3, 0:NB] = lists[...]
    across = jnp.broadcast_to(meta[0:1].astype(F32), (BLK, BLK))
    order = lax.broadcasted_iota(jnp.int32, (BLK, BLK), 0)
    meta[3:4] = jnp.min(jnp.where(across == across.T, order, NB), axis=0, keepdims=True)

    for o, copy in list(zip(Y_OFF, a2))[::-1][:4]:
        copy.wait_recv()
        share(a_in, at("y", -o), o)
    for o, copy in list(zip(Z_OFF, b2))[::-1]:
        copy.wait_recv()
        share(b_in, at("zh", -o), 8 + o)
    for o, copy in list(zip(Y_OFF, a2))[:3][::-1]:
        copy.wait_recv()
        share(a_in, at("y", -o), o)
    for copy in shared:
        copy.wait()

    @pl.loop(0, 8)
    def _(t):
        for i in range(8):
            core, yy, zz = t // 4, (t % 4) * 2 + i // 4, i % 4
            lanes = slice(i * BLK, (i + 1) * BLK)
            w[t, i * SUB : (i + 1) * SUB, lanes] = a_in[core, yy, zz, 0:SUB]
            w[t, BLK + i * SUB : BLK + (i + 1) * SUB, lanes] = a_in[core, yy, zz, SUB:]
            dn[t, i * SUB : (i + 1) * SUB, lanes] = b_in[core, zz, yy]

    for copy in a1 + b1 + a2 + b2:
        copy.wait_send()


def gathered(*args):
    hbm = pl.BlockSpec(memory_space=pltpu.HBM)
    vmem = pl.BlockSpec(memory_space=pltpu.VMEM)
    return pl.pallas_call(
        gather_kernel,
        name="gather_blocks",
        out_shape=(
            jax.ShapeDtypeStruct((8, 256, 1024), BF16),
            jax.ShapeDtypeStruct((8, 128, 1024), BF16),
            jax.ShapeDtypeStruct((TOK, D), BF16),
            jax.ShapeDtypeStruct((TOK, D), BF16),
            jax.ShapeDtypeStruct((8, BLK), jnp.int32),
        ),
        in_specs=[hbm] * 8,
        out_specs=(vmem,) * 5,
        scratch_shapes=[
            pltpu.VMEM((2, 8, 4, 2 * SUB, BLK), BF16),
            pltpu.VMEM((2, 4, 8, SUB, BLK), BF16),
            pltpu.VMEM((2 * SUB, BLK), BF16),
            pltpu.VMEM((SUB, BLK), BF16),
            pltpu.VMEM((2, BLK, BLK), BF16),
            pltpu.VMEM((3, NB), jnp.int32),
            pltpu.SemaphoreType.DMA((24,)),
            pltpu.SemaphoreType.DMA((24,)),
            pltpu.SemaphoreType.DMA((12,)),
            pltpu.SemaphoreType.DMA((12,)),
            pltpu.SemaphoreType.DMA((8,)),
        ],
        compiler_params=pltpu.CompilerParams(
            collective_id=0, has_side_effects=True, vmem_limit_bytes=32 << 20
        ),
    )(*args)


def place_of(k):
    return ((k & 1) << 5) | (((k >> 1) & 7) << 2) | (k >> 4)


def dot_nt(a, b):
    return lax.dot_general(a, b, (((1,), (1,)), ((), ())), preferred_element_type=F32)


def dot(a, b):
    return jnp.dot(a, b, preferred_element_type=F32)


def compute_kernel(
    w, dn, tok, cot, meta, part, wa, wb, acc, g_s, u_s, h_s, table, pairs, sem
):
    load = pltpu.make_async_copy(meta, table, sem)
    load.start()
    load.wait()

    def columns(ref, row):
        return ref[:, pl.ds(pl.multiple_of(row * BLK, BLK), BLK)]

    def flat(t, i):
        return (i % 4) * 16 + (((t & 3) * 2 + i // 4) * 2) + (t >> 2)

    @pl.loop(0, 8)
    def _(t):
        acc[pl.ds(t * 4, 4)] = jnp.zeros((4, TOK, BLK), F32)
        ks = [flat(t, i) for i in range(8)]
        gu = dot_nt(jnp.concatenate([columns(tok, table[1, k]) for k in ks], axis=1), w[t])
        g_s[t] = gu[:, :BLK]
        u_s[t] = gu[:, BLK:]
        h_s[t] = dot_nt(jnp.concatenate([columns(cot, table[2, k]) for k in ks], axis=1), dn[t])

    count = jnp.int32(0)
    for k in range(NB):
        first = table[3, k]
        pairs[count] = place_of(k) | (place_of(first) << 8)
        count = count + (first != k).astype(jnp.int32)
    group = lax.broadcasted_iota(jnp.int32, (TOK, BLK), 1) // SUB

    @pl.loop(0, count)
    def _(n):
        p, q = pairs[n] & 255, pairs[n] >> 8
        shift = ((q - p) * SUB) & (BLK - 1)
        for s in (g_s, u_s, h_s):
            moved = pltpu.roll(s[p >> 3], shift, axis=1)
            s[q >> 3] += jnp.where(group == (q & 7), moved, 0.0)

    @pl.loop(0, count)
    def _(n):
        p, q = pairs[n] & 255, pairs[n] >> 8
        shift = ((p - q) * SUB) & (BLK - 1)
        for s in (g_s, u_s, h_s):
            moved = pltpu.roll(s[q >> 3], shift, axis=1)
            s[p >> 3] = jnp.where(group == (p & 7), moved, s[p >> 3])

    @pl.loop(0, 8)
    def _(t):
        gate, up, hg = g_s[t], u_s[t], h_s[t]
        sig = jax.nn.sigmoid(gate)
        act = gate * sig
        hid = (act * up).T.astype(BF16)
        gg = hg * up * sig * (1.0 + gate * (1.0 - sig))
        ug = hg * act
        ggt, ugt = gg.T.astype(BF16), ug.T.astype(BF16)
        spread = dot(jnp.concatenate([gg.astype(BF16), ug.astype(BF16)], axis=1), w[t])
        for i in range(8):
            acc[table[1, flat(t, i)]] += spread[:, i * BLK : (i + 1) * BLK]
        core = t >> 2
        for j in range(4):
            rows = slice(32 * j, 32 * j + 32)
            ks = [flat(t, 2 * j), flat(t, 2 * j + 1)]
            left = jnp.concatenate([ggt[rows], ugt[rows]], axis=0)
            r = dot(left, jnp.concatenate([columns(tok, table[1, k]) for k in ks], axis=1))
            d = dot(hid[rows], jnp.concatenate([columns(cot, table[2, k]) for k in ks], axis=1))
            for n in range(2):
                i = 2 * j + n
                yy, zz = (t & 3) * 2 + i // 4, i % 4
                lanes = slice(n * BLK, (n + 1) * BLK)
                wa[core, yy, zz, 0:SUB] = r[n * SUB : (n + 1) * SUB, lanes]
                wa[core, yy, zz, SUB:] = r[32 + n * SUB : 32 + (n + 1) * SUB, lanes]
                wb[core, zz, yy] = d[n * SUB : (n + 1) * SUB, lanes]

    for m in range(8):
        for j in range(4):
            part[m, :, j * BLK : (j + 1) * BLK] = acc[4 * m + j].astype(BF16)


def computed(*args):
    vmem = pl.BlockSpec(memory_space=pltpu.VMEM)
    return pl.pallas_call(
        compute_kernel,
        name="block_grads",
        out_shape=(
            jax.ShapeDtypeStruct((8, TOK, 512), BF16),
            jax.ShapeDtypeStruct((2, 8, 4, 2 * SUB, BLK), F32),
            jax.ShapeDtypeStruct((2, 4, 8, SUB, BLK), F32),
        ),
        in_specs=[vmem] * 5,
        out_specs=(vmem,) * 3,
        scratch_shapes=[
            pltpu.VMEM((32, TOK, BLK), F32),
            pltpu.VMEM((8, TOK, BLK), F32),
            pltpu.VMEM((8, TOK, BLK), F32),
            pltpu.VMEM((8, TOK, BLK), F32),
            pltpu.SMEM((8, BLK), jnp.int32),
            pltpu.SMEM((BLK,), jnp.int32),
            pltpu.SemaphoreType.DMA,
        ],
        compiler_params=pltpu.CompilerParams(vmem_limit_bytes=24 << 20),
    )(*args)


def reduce_kernel(
    part, wa, wb, ig_in, fin,
    mid, sib_a, sib_b, sum_a, sum_b, in_a1, in_b1, sum_a2, sum_b2, in_a2, in_b2,
    s_sem, r_sem, s_mp, r_mp, s_fin, r_fin,
):
    c, z, y = lax.axis_index("c"), lax.axis_index("zh"), lax.axis_index("y")
    x, zl = lax.axis_index("x"), lax.axis_index("zl")
    m = x * 2 + zl
    enter(
        [{"zh": at("zh", o)} for o in Z_OFF]
        + [{"y": at("y", o)} for o in Y_OFF]
        + [sibling()]
        + [mp_peer(o) for o in MP_OFF]
    )
    o = 1 - c
    sib = [
        send(wa.at[o], sib_a, s_sem.at[0], r_sem.at[0], sibling()),
        send(wb.at[o], sib_b, s_sem.at[8], r_sem.at[8], sibling()),
    ]
    exch = []
    for h in range(2):
        for i, off in enumerate(X_OFF):
            q = at("x", off)
            n = h * 3 + i
            chunk = q * 2 + (1 - zl if h == 0 else zl)
            exch.append(send(part.at[chunk], ig_in.at[n], s_mp.at[n], r_mp.at[n], {"x": q}))
    sib[0].wait_recv()
    sum_a[...] = (wa[c] + sib_a[...]).astype(BF16)
    a1 = []
    for off in Y_OFF:
        q = at("y", off)
        a1.append(
            send(sum_a.at[q], in_a1.at[off], s_sem.at[16 + off], r_sem.at[16 + off], {"y": q})
        )
    sib[1].wait_recv()
    sum_b[...] = (wb[c] + sib_b[...]).astype(BF16)
    b1 = []
    for off in Z_OFF:
        q = at("zh", off)
        b1.append(
            send(sum_b.at[q], in_b1.at[off], s_sem.at[4 + off], r_sem.at[4 + off], {"zh": q})
        )
    total = sum_b[z].astype(F32)
    for off, copy in zip(Z_OFF, b1):
        copy.wait_recv()
        total += in_b1[off].astype(F32)
    sum_b2[...] = total.astype(BF16)
    b2 = []
    for off in Y_OFF:
        q = at("y", off)
        b2.append(
            send(sum_b2.at[q], in_b2.at[off], s_sem.at[8 + off], r_sem.at[8 + off], {"y": q})
        )
    total = sum_a[y].astype(F32)
    for off, copy in zip(Y_OFF, a1):
        copy.wait_recv()
        total += in_a1[off].astype(F32)
    sum_a2[...] = total.astype(BF16)
    a2 = []
    for off in Z_OFF:
        q = at("zh", off)
        a2.append(send(sum_a2.at[q], in_a2.at[off], s_sem.at[off], r_sem.at[off], {"zh": q}))
    total = part[x * 2 + 1 - zl].astype(F32)
    for i in range(3):
        exch[i].wait_recv()
        total += ig_in[i].astype(F32)
    mid[...] = total.astype(BF16)
    exch.append(send(mid, ig_in.at[6], s_mp.at[6], r_mp.at[6], {"zl": 1 - zl}))
    total = sum_b2[y].astype(F32)
    for off, copy in zip(Y_OFF, b2):
        copy.wait_recv()
        total += in_b2[off].astype(F32)
    fin[m, 2 * SUB :] = total.astype(fin.dtype)
    total = sum_a2[z].astype(F32)
    for off, copy in zip(Z_OFF, a2):
        copy.wait_recv()
        total += in_a2[off].astype(F32)
    fin[m, 0 : 2 * SUB] = total.astype(fin.dtype)
    last = [
        send(fin.at[m], fin.at[m], s_fin.at[i], r_fin.at[i], mp_peer(off))
        for i, off in enumerate(MP_OFF)
    ]
    for copy in exch[3:] + last:
        copy.wait_recv()
    for copy in sib + exch + a1 + b1 + a2 + b2 + last:
        copy.wait_send()


def reduced(part, wa, wb):
    vmem = pl.BlockSpec(memory_space=pltpu.VMEM)
    return pl.pallas_call(
        reduce_kernel,
        name="sum_grads",
        out_shape=(
            jax.ShapeDtypeStruct((7, TOK, 512), BF16),
            jax.ShapeDtypeStruct((8, 3 * SUB, BLK), BF16),
        ),
        in_specs=[vmem] * 3,
        out_specs=(vmem,) * 2,
        scratch_shapes=[
            pltpu.VMEM((TOK, 512), BF16),
            pltpu.VMEM((8, 4, 2 * SUB, BLK), F32),
            pltpu.VMEM((4, 8, SUB, BLK), F32),
            pltpu.VMEM((8, 4, 2 * SUB, BLK), BF16),
            pltpu.VMEM((4, 8, SUB, BLK), BF16),
            pltpu.VMEM((8, 4, 2 * SUB, BLK), BF16),
            pltpu.VMEM((4, 8, SUB, BLK), BF16),
            pltpu.VMEM((4, 2 * SUB, BLK), BF16),
            pltpu.VMEM((8, SUB, BLK), BF16),
            pltpu.VMEM((4, 2 * SUB, BLK), BF16),
            pltpu.VMEM((8, SUB, BLK), BF16),
            pltpu.SemaphoreType.DMA((24,)),
            pltpu.SemaphoreType.DMA((24,)),
            pltpu.SemaphoreType.DMA((7,)),
            pltpu.SemaphoreType.DMA((7,)),
            pltpu.SemaphoreType.DMA((7,)),
            pltpu.SemaphoreType.DMA((7,)),
        ],
        compiler_params=pltpu.CompilerParams(
            collective_id=1, has_side_effects=True, vmem_limit_bytes=32 << 20
        ),
    )(part, wa, wb)


def finish_kernel(part, ig_in, fin, ig_out, g_out, u_out, d_out):
    total = part[lax.axis_index("x") * 2 + lax.axis_index("zl")].astype(F32)
    for i in range(3, 7):
        total += ig_in[i].astype(F32)
    ig_out[...] = total.astype(BF16)
    scale = 9216**-0.5
    g_out[0] = fin[:, 0:SUB].astype(F32).reshape(BLK, BLK).T * scale
    u_out[0] = fin[:, SUB : 2 * SUB].astype(F32).reshape(BLK, BLK).T * scale
    d_out[0] = fin[:, 2 * SUB :].astype(F32).reshape(BLK, BLK) * scale


def finished(part, ig_in, fin):
    vmem = pl.BlockSpec(memory_space=pltpu.VMEM)
    grad = jax.ShapeDtypeStruct((1, BLK, BLK), F32)
    return pl.pallas_call(
        finish_kernel,
        name="write_grads",
        out_shape=(jax.ShapeDtypeStruct((TOK, 512), BF16), grad, grad, grad),
        in_specs=[vmem] * 3,
        out_specs=(vmem,) * 4,
        compiler_params=pltpu.CompilerParams(vmem_limit_bytes=16 << 20),
    )(part, ig_in, fin)


def on_device(tokens, cotangent, gate, up, down, col_block, in_row, out_row):
    args = (gate, up, down, tokens, cotangent, col_block, in_row, out_row)
    tiles = gathered(*(pltpu.with_memory_space_constraint(a, pltpu.HBM) for a in args))
    part, wa, wb = computed(*tiles)
    return finished(part, *reduced(part, wa, wb))


def solution(mesh):
    fine = Mesh(mesh.devices.reshape(4, 8, 2, 4, 2), AXES)
    dp, mp = ("zh", "y", "c"), ("x", "zl")
    return jax.shard_map(
        on_device,
        mesh=fine,
        in_specs=(P(dp, None), P(dp, None), P(dp), P(dp), P(dp), P(), P(), P()),
        out_specs=(P(dp, mp), P(dp), P(dp), P(dp)),
        check_vma=False,
    )
```

time: 82.9 us -> 61.7 us (0.74)
  the two profiles are of different devices: /device:TPU:8 before, /device:TPU:1 now
where the time goes in v2:
time: 61.7 us; the launch traced here: 61.1 us
  Pallas kernels  60.4 us (98%)
  between operations  0.66 us (1%)
    pallas_call x1, Pallas kernels, gathered(): pl.pallas_call(gather_kernel, name='gather_blocks', out_shape=(jax.ShapeD...  27.2 us
    pallas_call x1, Pallas kernels, reduced(): pl.pallas_call(reduce_kernel, name='sum_grads', out_shape=(jax.ShapeDtype...  23.5 us
    pallas_call x1, Pallas kernels, computed(): pl.pallas_call(compute_kernel, name='block_grads', out_shape=(jax.ShapeDt...  8.94 us

profile of v2, /device:TPU:1, one launch (start us, length us, event | category | flops | bytes accessed | tf_op | source)
XLA Modules:
  0.0 61.1 jit_solution(17759382296094234838)
XLA Ops:
  0.6 27.2 %gather_blocks.1 = (bf16[8,256,1024]{2,1,0:T(8,128)(2,1)S(1)}, bf16[8,128,1024]{2,1,0:T(8,128)(2,1)S(1)}, bf16[144,4096]{1,0:T(8,128)(2,1)S(1)}, bf16[144,4096]{1,0:T(8,128)(2,1)S(1)}, s32[8,128]{1,0:T(8,128)S(1)}) custom-call(bf16[1,128,128]{2,1,0:T(8,128)(2,1)} %gate.1, bf16[1,128,128]{2,1,0:T(8,128)(2,1)} %up.1, bf16[1,128,128]{2,1,0:T(8,128)(2,1)} %down.1, ...), custom_call_target="tpu_custom_call" | custom-call | tf_op jit(solution)/shard_map/gather_blocks/pallas_call | solution.py:162
  27.8 8.9 %block_grads.1 = (bf16[8,144,512]{2,1,0:T(8,128)(2,1)S(1)}, f32[2,8,4,32,128]{4,3,2,1,0:T(8,128)S(1)}, f32[2,4,8,16,128]{4,3,2,1,0:T(8,128)S(1)}) custom-call(bf16[8,256,1024]{2,1,0:T(8,128)(2,1)S(1)} %get-tuple-element.14.w, bf16[8,128,1024]{2,1,0:T(8,128)(2,1)S(1)} %get-tuple-element.15.dn, bf16[144,4096]{1,0:T(8,128)(2,1)S(1)} %get-tuple-element.16.tok, ...), custom_call_target="tpu_custom_call" | custom-call | tf_op jit(solution)/shard_map/block_grads/pallas_call | solution.py:284
  36.8 23.5 %sum_grads.1 = (bf16[7,144,512]{2,1,0:T(8,128)(2,1)S(1)}, bf16[8,48,128]{2,1,0:T(8,128)(2,1)S(1)}) custom-call(bf16[8,144,512]{2,1,0:T(8,128)(2,1)S(1)} %get-tuple-element.19.part, f32[2,8,4,32,128]{4,3,2,1,0:T(8,128)S(1)} %get-tuple-element.20.wa, f32[2,4,8,16,128]{4,3,2,1,0:T(8,128)S(1)} %get-tuple-element.21.wb), custom_call_target="tpu_custom_call" | custom-call | tf_op jit(solution)/shard_map/sum_grads/pallas_call | solution.py:397
  60.2 0.8 %write_grads.1 = (bf16[144,512]{1,0:T(8,128)(2,1)}, f32[1,128,128]{2,1,0:T(8,128)}, f32[1,128,128]{2,1,0:T(8,128)}, f32[1,128,128]{2,1,0:T(8,128)}) custom-call(bf16[8,144,512]{2,1,0:T(8,128)(2,1)S(1)} %get-tuple-element.19.part, bf16[7,144,512]{2,1,0:T(8,128)(2,1)S(1)} %get-tuple-element.22.ig_in, bf16[8,48,128]{2,1,0:T(8,128)(2,1)S(1)} %get-tuple-element.23.fin), custom_call_target="tpu_custom_call" | custom-call | tf_op jit(solution)/shard_map/write_grads/pallas_call | solution.py:445

commit v3 on v2

--- a/solution.py
+++ b/solution.py
@@ -48,12 +48,38 @@
     return copy
 
 
+OFF = {"y": Y_OFF, "zh": Z_OFF}
+OTHER = {"y": "zh", "zh": "y"}
+GATHER_FIRST = (("zh", "y"), ("y", "zh"))
+REDUCE_FIRST = (("y", "zh"), ("zh", "y"))
+
+
+def line(ref, axis, q):
+    return ref.at[q] if axis == "y" else ref.at[pl.ds(0, SIZE["y"]), q]
+
+
+def flat(t, i):
+    return (i % 4) * 16 + (((t & 3) * 2 + i // 4) * 2) + (t >> 2)
+
+
+def columns(ref, row):
+    return ref[:, pl.ds(pl.multiple_of(row * BLK, BLK), BLK)]
+
+
+def forward(t, tok, cot, in_row, out_row, w, dn):
+    ks = [flat(t, i) for i in range(8)]
+    gu = dot_nt(jnp.concatenate([columns(tok, in_row(k)) for k in ks], axis=1), w[t])
+    hg = dot_nt(jnp.concatenate([columns(cot, out_row(k)) for k in ks], axis=1), dn[t])
+    return gu[:, :BLK], gu[:, BLK:], hg
+
+
 def gather_kernel(
     gate, up, down, tok, cot, col, in_row, out_row,
     w, dn, tok_v, cot_v, meta,
     a_in, b_in, own_a, own_b, raw, lists, s_sem, r_sem, s_sib, r_sib, local,
 ):
     c, z, y = lax.axis_index("c"), lax.axis_index("zh"), lax.axis_index("y")
+    here = {"y": y, "zh": z}
     rows = pl.ds((lax.axis_index("x") * 2 + lax.axis_index("zl")) * SUB, SUB)
     partners = (
         [{"zh": at("zh", o)} for o in Z_OFF] + [{"y": at("y", o)} for o in Y_OFF] + [sibling()]
@@ -88,72 +114,100 @@
         own_a[i * SUB : (i + 1) * SUB] = raw[i, rows]
     loads[2].wait()
     a_in[c, y, z] = own_a[...]
-    b_in[c, z, y] = own_b[...]
-    pl.semaphore_wait(barrier, len(partners))
-    a1 = [
-        send(own_a, a_in.at[c, y, z], s_sem.at[o], r_sem.at[o], {"zh": at("zh", o)})
-        for o in Z_OFF
-    ]
-    b1 = [
-        send(own_b, b_in.at[c, z, y], s_sem.at[8 + o], r_sem.at[8 + o], {"y": at("y", o)})
-        for o in Y_OFF
-    ]
-    for copy in a1:
-        copy.wait_recv()
-    a2 = [
-        send(a_in.at[c, y], a_in.at[c, y], s_sem.at[16 + o], r_sem.at[16 + o], {"y": at("y", o)})
-        for o in Y_OFF
-    ]
-    for copy in b1:
-        copy.wait_recv()
-    b2 = [
-        send(b_in.at[c, z], b_in.at[c, z], s_sem.at[4 + o], r_sem.at[4 + o], {"zh": at("zh", o)})
-        for o in Z_OFF
-    ]
-    shared = []
-
-    def share(ref, index, slot):
-        part = ref.at[c, index]
-        shared.append(send(part, part, s_sib.at[slot], r_sib.at[slot], sibling()))
-
-    share(a_in, y, 0)
-    share(b_in, z, 8)
+    b_in[c, y, z] = own_b[...]
 
     @pl.loop(0, 8)
     def _(t):
         w[t] = jnp.zeros_like(w[t])
         dn[t] = jnp.zeros_like(dn[t])
 
-    for copy in loads[3:]:
+    for copy in loads[3:6]:
         copy.wait()
     meta[0:3, 0:NB] = lists[...]
     across = jnp.broadcast_to(meta[0:1].astype(F32), (BLK, BLK))
     order = lax.broadcasted_iota(jnp.int32, (BLK, BLK), 0)
     meta[3:4] = jnp.min(jnp.where(across == across.T, order, NB), axis=0, keepdims=True)
-
-    for o, copy in list(zip(Y_OFF, a2))[::-1][:4]:
-        copy.wait_recv()
-        share(a_in, at("y", -o), o)
-    for o, copy in list(zip(Z_OFF, b2))[::-1]:
-        copy.wait_recv()
-        share(b_in, at("zh", -o), 8 + o)
-    for o, copy in list(zip(Y_OFF, a2))[:3][::-1]:
-        copy.wait_recv()
-        share(a_in, at("y", -o), o)
-    for copy in shared:
-        copy.wait()
-
-    @pl.loop(0, 8)
-    def _(t):
+    pl.semaphore_wait(barrier, len(partners))
+
+    def lay(t):
+        core = t >> 2
         for i in range(8):
-            core, yy, zz = t // 4, (t % 4) * 2 + i // 4, i % 4
+            yy, zz = (t & 3) * 2 + i // 4, i % 4
             lanes = slice(i * BLK, (i + 1) * BLK)
             w[t, i * SUB : (i + 1) * SUB, lanes] = a_in[core, yy, zz, 0:SUB]
             w[t, BLK + i * SUB : BLK + (i + 1) * SUB, lanes] = a_in[core, yy, zz, SUB:]
-            dn[t, i * SUB : (i + 1) * SUB, lanes] = b_in[core, zz, yy]
-
-    for copy in a1 + b1 + a2 + b2:
-        copy.wait_send()
+            dn[t, i * SUB : (i + 1) * SUB, lanes] = b_in[core, yy, zz]
+
+    def on_core(core):
+        parts = []
+        for n, (own, buf) in enumerate(((own_a, a_in), (own_b, b_in))):
+            first = GATHER_FIRST[core][n]
+            parts.append((first, own, buf.at[core], buf.at[1 - core], n))
+        parts.sort(key=lambda p: p[0])
+
+        def cross(axis, n, o, src, dst):
+            i = n * 16 + (8 if axis == "zh" else 0) + o
+            return send(src, dst, s_sem.at[i], r_sem.at[i], {axis: at(axis, o)})
+
+        one, two, shared = {}, {}, []
+        for first, own, buf, _, n in parts:
+            one[n] = [cross(first, n, o, own, buf.at[y, z]) for o in OFF[first]]
+
+        def share(axis, buf, o, n):
+            part = line(buf, axis, at(axis, -o))
+            i = n * 8 + o
+            shared.append(send(part, part, s_sib.at[i], r_sib.at[i], sibling()))
+
+        for first, _, buf, _, n in parts[::-1]:
+            for copy in one[n]:
+                copy.wait_recv()
+            held = line(buf, OTHER[first], here[OTHER[first]])
+            two[n] = [cross(OTHER[first], n, o, held, held) for o in OFF[OTHER[first]]]
+            share(OTHER[first], buf, 0, n)
+        (_, _, z_buf, _, zn), (_, _, y_buf, _, yn) = parts
+        arrivals = list(zip(Y_OFF, two[yn]))[::-1]
+        for o, copy in arrivals[:4]:
+            copy.wait_recv()
+            share("y", y_buf, o, yn)
+        for o, copy in list(zip(Z_OFF, two[zn]))[::-1]:
+            copy.wait_recv()
+            share("zh", z_buf, o, zn)
+        for o, copy in arrivals[4:]:
+            copy.wait_recv()
+            share("y", y_buf, o, yn)
+        for copy in shared + one[0] + one[1] + two[0] + two[1]:
+            copy.wait_send()
+
+    def from_sibling(core):
+        for n, buf in enumerate((a_in, b_in)):
+            axis = OTHER[GATHER_FIRST[1 - core][n]]
+            for o in (0, *OFF[axis]):
+                part = line(buf.at[1 - core], axis, at(axis, -o))
+                i = n * 8 + o
+                pltpu.make_async_remote_copy(
+                    src_ref=part,
+                    dst_ref=part,
+                    send_sem=s_sib.at[i],
+                    recv_sem=r_sib.at[i],
+                    device_id=sibling(),
+                    device_id_type=MESH_ID,
+                ).wait_recv()
+
+    for core in range(2):
+        pl.when(c == core)(lambda core=core: on_core(core))
+    for copy in loads[6:]:
+        copy.wait()
+
+    @pl.loop(0, 4)
+    def _(j):
+        lay(c * 4 + j)
+
+    for core in range(2):
+        pl.when(c == core)(lambda core=core: from_sibling(core))
+
+    @pl.loop(0, 4)
+    def _(j):
+        lay((1 - c) * 4 + j)
 
 
 def gathered(*args):
@@ -173,19 +227,19 @@
         out_specs=(vmem,) * 5,
         scratch_shapes=[
             pltpu.VMEM((2, 8, 4, 2 * SUB, BLK), BF16),
-            pltpu.VMEM((2, 4, 8, SUB, BLK), BF16),
+            pltpu.VMEM((2, 8, 4, SUB, BLK), BF16),
             pltpu.VMEM((2 * SUB, BLK), BF16),
             pltpu.VMEM((SUB, BLK), BF16),
             pltpu.VMEM((2, BLK, BLK), BF16),
             pltpu.VMEM((3, NB), jnp.int32),
-            pltpu.SemaphoreType.DMA((24,)),
-            pltpu.SemaphoreType.DMA((24,)),
-            pltpu.SemaphoreType.DMA((12,)),
-            pltpu.SemaphoreType.DMA((12,)),
+            pltpu.SemaphoreType.DMA((32,)),
+            pltpu.SemaphoreType.DMA((32,)),
+            pltpu.SemaphoreType.DMA((16,)),
+            pltpu.SemaphoreType.DMA((16,)),
             pltpu.SemaphoreType.DMA((8,)),
         ],
         compiler_params=pltpu.CompilerParams(
-            collective_id=0, has_side_effects=True, vmem_limit_bytes=32 << 20
+            collective_id=0, has_side_effects=True, vmem_limit_bytes=24 << 20
         ),
     )(*args)
 
@@ -209,20 +263,11 @@
     load.start()
     load.wait()
 
-    def columns(ref, row):
-        return ref[:, pl.ds(pl.multiple_of(row * BLK, BLK), BLK)]
-
-    def flat(t, i):
-        return (i % 4) * 16 + (((t & 3) * 2 + i // 4) * 2) + (t >> 2)
-
-    @pl.loop(0, 8)
+    @pl.loop(0, 8, unroll=2)
     def _(t):
         acc[pl.ds(t * 4, 4)] = jnp.zeros((4, TOK, BLK), F32)
-        ks = [flat(t, i) for i in range(8)]
-        gu = dot_nt(jnp.concatenate([columns(tok, table[1, k]) for k in ks], axis=1), w[t])
-        g_s[t] = gu[:, :BLK]
-        u_s[t] = gu[:, BLK:]
-        h_s[t] = dot_nt(jnp.concatenate([columns(cot, table[2, k]) for k in ks], axis=1), dn[t])
+        rows_of = (lambda k: table[1, k]), (lambda k: table[2, k])
+        g_s[t], u_s[t], h_s[t] = forward(t, tok, cot, *rows_of, w, dn)
 
     count = jnp.int32(0)
     for k in range(NB):
@@ -247,7 +292,7 @@
             moved = pltpu.roll(s[q >> 3], shift, axis=1)
             s[p >> 3] = jnp.where(group == (p & 7), moved, s[p >> 3])
 
-    @pl.loop(0, 8)
+    @pl.loop(0, 8, unroll=2)
     def _(t):
         gate, up, hg = g_s[t], u_s[t], h_s[t]
         sig = jax.nn.sigmoid(gate)
@@ -272,7 +317,7 @@
                 lanes = slice(n * BLK, (n + 1) * BLK)
                 wa[core, yy, zz, 0:SUB] = r[n * SUB : (n + 1) * SUB, lanes]
                 wa[core, yy, zz, SUB:] = r[32 + n * SUB : 32 + (n + 1) * SUB, lanes]
-                wb[core, zz, yy] = d[n * SUB : (n + 1) * SUB, lanes]
+                wb[core, yy, zz] = d[n * SUB : (n + 1) * SUB, lanes]
 
     for m in range(8):
         for j in range(4):
@@ -287,7 +332,7 @@
         out_shape=(
             jax.ShapeDtypeStruct((8, TOK, 512), BF16),
             jax.ShapeDtypeStruct((2, 8, 4, 2 * SUB, BLK), F32),
-            jax.ShapeDtypeStruct((2, 4, 8, SUB, BLK), F32),
+            jax.ShapeDtypeStruct((2, 8, 4, SUB, BLK), F32),
         ),
         in_specs=[vmem] * 5,
         out_specs=(vmem,) * 3,
@@ -306,11 +351,13 @@
 
 def reduce_kernel(
     part, wa, wb, ig_in, fin,
-    mid, sib_a, sib_b, sum_a, sum_b, in_a1, in_b1, sum_a2, sum_b2, in_a2, in_b2,
-    s_sem, r_sem, s_mp, r_mp, s_fin, r_fin,
+    mid, sib_a, sib_b, sum_a, sum_b, ya, yb, za, zb, y2a, y2b, z2a, z2b,
+    in_y2a, in_y2b, in_z2a, in_z2b,
+    s_sem, r_sem, s_sib, r_sib, s_mp, r_mp, s_fin, r_fin,
 ):
     c, z, y = lax.axis_index("c"), lax.axis_index("zh"), lax.axis_index("y")
     x, zl = lax.axis_index("x"), lax.axis_index("zl")
+    here = {"y": y, "zh": z}
     m = x * 2 + zl
     enter(
         [{"zh": at("zh", o)} for o in Z_OFF]
@@ -318,82 +365,109 @@
         + [sibling()]
         + [mp_peer(o) for o in MP_OFF]
     )
-    o = 1 - c
-    sib = [
-        send(wa.at[o], sib_a, s_sem.at[0], r_sem.at[0], sibling()),
-        send(wb.at[o], sib_b, s_sem.at[8], r_sem.at[8], sibling()),
-    ]
-    exch = []
-    for h in range(2):
-        for i, off in enumerate(X_OFF):
-            q = at("x", off)
-            n = h * 3 + i
-            chunk = q * 2 + (1 - zl if h == 0 else zl)
-            exch.append(send(part.at[chunk], ig_in.at[n], s_mp.at[n], r_mp.at[n], {"x": q}))
-    sib[0].wait_recv()
-    sum_a[...] = (wa[c] + sib_a[...]).astype(BF16)
-    a1 = []
-    for off in Y_OFF:
-        q = at("y", off)
-        a1.append(
-            send(sum_a.at[q], in_a1.at[off], s_sem.at[16 + off], r_sem.at[16 + off], {"y": q})
-        )
-    sib[1].wait_recv()
-    sum_b[...] = (wb[c] + sib_b[...]).astype(BF16)
-    b1 = []
-    for off in Z_OFF:
-        q = at("zh", off)
-        b1.append(
-            send(sum_b.at[q], in_b1.at[off], s_sem.at[4 + off], r_sem.at[4 + off], {"zh": q})
-        )
-    total = sum_b[z].astype(F32)
-    for off, copy in zip(Z_OFF, b1):
-        copy.wait_recv()
-        total += in_b1[off].astype(F32)
-    sum_b2[...] = total.astype(BF16)
-    b2 = []
-    for off in Y_OFF:
-        q = at("y", off)
-        b2.append(
-            send(sum_b2.at[q], in_b2.at[off], s_sem.at[8 + off], r_sem.at[8 + off], {"y": q})
-        )
-    total = sum_a[y].astype(F32)
-    for off, copy in zip(Y_OFF, a1):
-        copy.wait_recv()
-        total += in_a1[off].astype(F32)
-    sum_a2[...] = total.astype(BF16)
-    a2 = []
-    for off in Z_OFF:
-        q = at("zh", off)
-        a2.append(send(sum_a2.at[q], in_a2.at[off], s_sem.at[off], r_sem.at[off], {"zh": q}))
-    total = part[x * 2 + 1 - zl].astype(F32)
-    for i in range(3):
-        exch[i].wait_recv()
-        total += ig_in[i].astype(F32)
-    mid[...] = total.astype(BF16)
-    exch.append(send(mid, ig_in.at[6], s_mp.at[6], r_mp.at[6], {"zl": 1 - zl}))
-    total = sum_b2[y].astype(F32)
-    for off, copy in zip(Y_OFF, b2):
-        copy.wait_recv()
-        total += in_b2[off].astype(F32)
-    fin[m, 2 * SUB :] = total.astype(fin.dtype)
-    total = sum_a2[z].astype(F32)
-    for off, copy in zip(Z_OFF, a2):
-        copy.wait_recv()
-        total += in_a2[off].astype(F32)
-    fin[m, 0 : 2 * SUB] = total.astype(fin.dtype)
-    last = [
-        send(fin.at[m], fin.at[m], s_fin.at[i], r_fin.at[i], mp_peer(off))
-        for i, off in enumerate(MP_OFF)
-    ]
-    for copy in exch[3:] + last:
-        copy.wait_recv()
-    for copy in sib + exch + a1 + b1 + a2 + b2 + last:
-        copy.wait_send()
+    w, sib, acc = (wa, wb), (sib_a, sib_b), (sum_a, sum_b)
+    in1 = {"y": (ya, yb), "zh": (za, zb)}
+    sum2 = {"y": (y2a, y2b), "zh": (z2a, z2b)}
+    in2 = {"y": (in_y2a, in_y2b), "zh": (in_z2a, in_z2b)}
+    place = (pl.ds(0, 2 * SUB), pl.ds(2 * SUB, SUB))
+
+    def on_core(core):
+        mine = sorted((REDUCE_FIRST[core][n], n) for n in range(2))
+        theirs = sorted((REDUCE_FIRST[1 - core][n], n) for n in range(2))
+        sent, given = [], {}
+
+        def sib_copy(n, axis, o, owner):
+            i = n * 8 + o
+            q = at(axis, o)
+            return pltpu.make_async_remote_copy(
+                src_ref=line(w[n].at[owner], axis, q),
+                dst_ref=line(sib[n], axis, q),
+                send_sem=s_sib.at[i],
+                recv_sem=r_sib.at[i],
+                device_id=sibling(),
+                device_id_type=MESH_ID,
+            )
+
+        for axis, n in theirs:
+            for o in (*OFF[axis], 0):
+                copy = sib_copy(n, axis, o, 1 - core)
+                copy.start()
+                sent.append(copy)
+        exch = []
+        for h in range(2):
+            for i, off in enumerate(X_OFF):
+                q = at("x", off)
+                k = h * 3 + i
+                chunk = q * 2 + (1 - zl if h == 0 else zl)
+                exch.append(send(part.at[chunk], ig_in.at[k], s_mp.at[k], r_mp.at[k], {"x": q}))
+        for axis, n in mine:
+            given[n] = []
+            for o in (*OFF[axis], 0):
+                sib_copy(n, axis, o, core).wait_recv()
+                q = at(axis, o)
+                if axis == "y":
+                    acc[n][q] = (w[n][core, q] + sib[n][q]).astype(BF16)
+                else:
+                    acc[n][:, q] = (w[n][core, :, q] + sib[n][:, q]).astype(BF16)
+                if o:
+                    i = n * 32 + (8 if axis == "zh" else 0) + o
+                    given[n].append(
+                        send(
+                            line(acc[n], axis, q), in1[axis][n].at[o],
+                            s_sem.at[i], r_sem.at[i], {axis: q},
+                        )
+                    )
+        second = {}
+        for axis, n in mine[::-1]:
+            q = here[axis]
+            total = (acc[n][q] if axis == "y" else acc[n][:, q]).astype(F32)
+            for o, copy in zip(OFF[axis], given[n]):
+                copy.wait_recv()
+                total += in1[axis][n][o].astype(F32)
+            last_axis = OTHER[axis]
+            sum2[last_axis][n][...] = total.astype(BF16)
+            second[n] = []
+            for o in OFF[last_axis]:
+                i = n * 32 + 16 + (8 if last_axis == "zh" else 0) + o
+                q = at(last_axis, o)
+                second[n].append(
+                    send(
+                        sum2[last_axis][n].at[q], in2[last_axis][n].at[o],
+                        s_sem.at[i], r_sem.at[i], {last_axis: q},
+                    )
+                )
+        total = part[x * 2 + 1 - zl].astype(F32)
+        for i in range(3):
+            exch[i].wait_recv()
+            total += ig_in[i].astype(F32)
+        mid[...] = total.astype(BF16)
+        exch.append(send(mid, ig_in.at[6], s_mp.at[6], r_mp.at[6], {"zl": 1 - zl}))
+        for axis, n in mine[::-1]:
+            last_axis = OTHER[axis]
+            total = sum2[last_axis][n][here[last_axis]].astype(F32)
+            for o, copy in zip(OFF[last_axis], second[n]):
+                copy.wait_recv()
+                total += in2[last_axis][n][o].astype(F32)
+            fin[m, place[n]] = total.astype(fin.dtype)
+        last = [
+            send(fin.at[m], fin.at[m], s_fin.at[i], r_fin.at[i], mp_peer(off))
+            for i, off in enumerate(MP_OFF)
+        ]
+        for copy in exch[3:] + last:
+            copy.wait_recv()
+        for copy in sent + exch + given[0] + given[1] + second[0] + second[1] + last:
+            copy.wait_send()
+
+    for core in range(2):
+        pl.when(c == core)(lambda core=core: on_core(core))
 
 
 def reduced(part, wa, wb):
     vmem = pl.BlockSpec(memory_space=pltpu.VMEM)
+
+    def pair(*lead, kind=BF16):
+        return [pltpu.VMEM((*lead, 2 * SUB, BLK), kind), pltpu.VMEM((*lead, SUB, BLK), kind)]
+
     return pl.pallas_call(
         reduce_kernel,
         name="sum_grads",
@@ -405,18 +479,18 @@
         out_specs=(vmem,) * 2,
         scratch_shapes=[
             pltpu.VMEM((TOK, 512), BF16),
-            pltpu.VMEM((8, 4, 2 * SUB, BLK), F32),
-            pltpu.VMEM((4, 8, SUB, BLK), F32),
-            pltpu.VMEM((8, 4, 2 * SUB, BLK), BF16),
-            pltpu.VMEM((4, 8, SUB, BLK), BF16),
-            pltpu.VMEM((8, 4, 2 * SUB, BLK), BF16),
-            pltpu.VMEM((4, 8, SUB, BLK), BF16),
-            pltpu.VMEM((4, 2 * SUB, BLK), BF16),
-            pltpu.VMEM((8, SUB, BLK), BF16),
-            pltpu.VMEM((4, 2 * SUB, BLK), BF16),
-            pltpu.VMEM((8, SUB, BLK), BF16),
-            pltpu.SemaphoreType.DMA((24,)),
-            pltpu.SemaphoreType.DMA((24,)),
+            *pair(8, 4, kind=F32),
+            *pair(8, 4),
+            *pair(8, 4),
+            *pair(4, 8),
+            *pair(8),
+            *pair(4),
+            *pair(8),
+            *pair(4),
+            pltpu.SemaphoreType.DMA((64,)),
+            pltpu.SemaphoreType.DMA((64,)),
+            pltpu.SemaphoreType.DMA((16,)),
+            pltpu.SemaphoreType.DMA((16,)),
             pltpu.SemaphoreType.DMA((7,)),
             pltpu.SemaphoreType.DMA((7,)),
             pltpu.SemaphoreType.DMA((7,)),

time: 61.7 us -> 60 us (0.972)
  Pallas kernels: 60.4 us -> 58.5 us
    pallas_call x1, Pallas kernels: 8.94 us -> 7.27 us  [computed(): pl.pallas_call(compute_kernel, name='block_grads', out_shape=(jax.ShapeDt...]
    pallas_call x1, Pallas kernels: 27.2 us -> 26.4 us  [gathered(): pl.pallas_call(gather_kernel, name='gather_blocks', out_shape=(jax.ShapeD...]
where the time goes in v3:
time: 60 us; the launch traced here: 59.2 us
  Pallas kernels  58.5 us (98%)
  between operations  0.66 us (1%)
    pallas_call x1, Pallas kernels, gathered(): pl.pallas_call(gather_kernel, name='gather_blocks', out_shape=(jax.ShapeD...  26.4 us
    pallas_call x1, Pallas kernels, reduced(): pl.pallas_call(reduce_kernel, name='sum_grads', out_shape=(jax.ShapeDtype...  24 us
    pallas_call x1, Pallas kernels, computed(): pl.pallas_call(compute_kernel, name='block_grads', out_shape=(jax.ShapeDt...  7.27 us

profile of v3, /device:TPU:1, one launch (start us, length us, event | category | flops | bytes accessed | tf_op | source)
XLA Modules:
  0.0 59.2 jit_solution(6894592614975881712)
XLA Ops:
  0.6 26.4 %gather_blocks.1 = (bf16[8,256,1024]{2,1,0:T(8,128)(2,1)S(1)}, bf16[8,128,1024]{2,1,0:T(8,128)(2,1)S(1)}, bf16[144,4096]{1,0:T(8,128)(2,1)S(1)}, bf16[144,4096]{1,0:T(8,128)(2,1)S(1)}, s32[8,128]{1,0:T(8,128)S(1)}) custom-call(bf16[1,128,128]{2,1,0:T(8,128)(2,1)} %gate.1, bf16[1,128,128]{2,1,0:T(8,128)(2,1)} %up.1, bf16[1,128,128]{2,1,0:T(8,128)(2,1)} %down.1, ...), custom_call_target="tpu_custom_call" | custom-call | tf_op jit(solution)/shard_map/gather_blocks/pallas_call | solution.py:216
  27.0 7.3 %block_grads.1 = (bf16[8,144,512]{2,1,0:T(8,128)(2,1)S(1)}, f32[2,8,4,32,128]{4,3,2,1,0:T(8,128)S(1)}, f32[2,8,4,16,128]{4,3,2,1,0:T(8,128)S(1)}) custom-call(bf16[8,256,1024]{2,1,0:T(8,128)(2,1)S(1)} %get-tuple-element.14.w, bf16[8,128,1024]{2,1,0:T(8,128)(2,1)S(1)} %get-tuple-element.15.dn, bf16[144,4096]{1,0:T(8,128)(2,1)S(1)} %get-tuple-element.16.tok, ...), custom_call_target="tpu_custom_call" | custom-call | tf_op jit(solution)/shard_map/block_grads/pallas_call | solution.py:329
  34.3 24.0 %sum_grads.1 = (bf16[7,144,512]{2,1,0:T(8,128)(2,1)S(1)}, bf16[8,48,128]{2,1,0:T(8,128)(2,1)S(1)}) custom-call(bf16[8,144,512]{2,1,0:T(8,128)(2,1)S(1)} %get-tuple-element.19.part, f32[2,8,4,32,128]{4,3,2,1,0:T(8,128)S(1)} %get-tuple-element.20.wa, f32[2,8,4,16,128]{4,3,2,1,0:T(8,128)S(1)} %get-tuple-element.21.wb), custom_call_target="tpu_custom_call" | custom-call | tf_op jit(solution)/shard_map/sum_grads/pallas_call | solution.py:471
  58.4 0.8 %write_grads.1 = (bf16[144,512]{1,0:T(8,128)(2,1)}, f32[1,128,128]{2,1,0:T(8,128)}, f32[1,128,128]{2,1,0:T(8,128)}, f32[1,128,128]{2,1,0:T(8,128)}) custom-call(bf16[8,144,512]{2,1,0:T(8,128)(2,1)S(1)} %get-tuple-element.19.part, bf16[7,144,512]{2,1,0:T(8,128)(2,1)S(1)} %get-tuple-element.22.ig_in, bf16[8,48,128]{2,1,0:T(8,128)(2,1)S(1)} %get-tuple-element.23.fin), custom_call_target="tpu_custom_call" | custom-call | tf_op jit(solution)/shard_map/write_grads/pallas_call | solution.py:519

commit v4 on v3

--- a/solution.py
+++ b/solution.py
@@ -116,18 +116,20 @@
     a_in[c, y, z] = own_a[...]
     b_in[c, y, z] = own_b[...]
 
-    @pl.loop(0, 8)
-    def _(t):
-        w[t] = jnp.zeros_like(w[t])
-        dn[t] = jnp.zeros_like(dn[t])
-
-    for copy in loads[3:6]:
-        copy.wait()
-    meta[0:3, 0:NB] = lists[...]
-    across = jnp.broadcast_to(meta[0:1].astype(F32), (BLK, BLK))
-    order = lax.broadcasted_iota(jnp.int32, (BLK, BLK), 0)
-    meta[3:4] = jnp.min(jnp.where(across == across.T, order, NB), axis=0, keepdims=True)
     pl.semaphore_wait(barrier, len(partners))
+
+    def prepare():
+        @pl.loop(0, 8)
+        def _(t):
+            w[t] = jnp.zeros_like(w[t])
+            dn[t] = jnp.zeros_like(dn[t])
+
+        for copy in loads[3:6]:
+            copy.wait()
+        meta[0:3, 0:NB] = lists[...]
+        across = jnp.broadcast_to(meta[0:1].astype(F32), (BLK, BLK))
+        order = lax.broadcasted_iota(jnp.int32, (BLK, BLK), 0)
+        meta[3:4] = jnp.min(jnp.where(across == across.T, order, NB), axis=0, keepdims=True)
 
     def lay(t):
         core = t >> 2
@@ -152,6 +154,8 @@
         one, two, shared = {}, {}, []
         for first, own, buf, _, n in parts:
             one[n] = [cross(first, n, o, own, buf.at[y, z]) for o in OFF[first]]
+
+        prepare()
 
         def share(axis, buf, o, n):
             part = line(buf, axis, at(axis, -o))
@@ -263,7 +267,7 @@
     load.start()
     load.wait()
 
-    @pl.loop(0, 8, unroll=2)
+    @pl.loop(0, 8, unroll=8)
     def _(t):
         acc[pl.ds(t * 4, 4)] = jnp.zeros((4, TOK, BLK), F32)
         rows_of = (lambda k: table[1, k]), (lambda k: table[2, k])
@@ -292,7 +296,7 @@
             moved = pltpu.roll(s[q >> 3], shift, axis=1)
             s[p >> 3] = jnp.where(group == (p & 7), moved, s[p >> 3])
 
-    @pl.loop(0, 8, unroll=2)
+    @pl.loop(0, 8, unroll=8)
     def _(t):
         gate, up, hg = g_s[t], u_s[t], h_s[t]
         sig = jax.nn.sigmoid(gate)
@@ -315,9 +319,9 @@
                 i = 2 * j + n
                 yy, zz = (t & 3) * 2 + i // 4, i % 4
                 lanes = slice(n * BLK, (n + 1) * BLK)
-                wa[core, yy, zz, 0:SUB] = r[n * SUB : (n + 1) * SUB, lanes]
-                wa[core, yy, zz, SUB:] = r[32 + n * SUB : 32 + (n + 1) * SUB, lanes]
-                wb[core, yy, zz] = d[n * SUB : (n + 1) * SUB, lanes]
+                wa[core, yy, zz, 0:SUB] = r[n * SUB : (n + 1) * SUB, lanes].astype(BF16)
+                wa[core, yy, zz, SUB:] = r[32 + n * SUB : 48 + n * SUB, lanes].astype(BF16)
+                wb[core, yy, zz] = d[n * SUB : (n + 1) * SUB, lanes].astype(BF16)
 
     for m in range(8):
         for j in range(4):
@@ -331,8 +335,8 @@
         name="block_grads",
         out_shape=(
             jax.ShapeDtypeStruct((8, TOK, 512), BF16),
-            jax.ShapeDtypeStruct((2, 8, 4, 2 * SUB, BLK), F32),
-            jax.ShapeDtypeStruct((2, 8, 4, SUB, BLK), F32),
+            jax.ShapeDtypeStruct((2, 8, 4, 2 * SUB, BLK), BF16),
+            jax.ShapeDtypeStruct((2, 8, 4, SUB, BLK), BF16),
         ),
         in_specs=[vmem] * 5,
         out_specs=(vmem,) * 3,
@@ -347,6 +351,10 @@
         ],
         compiler_params=pltpu.CompilerParams(vmem_limit_bytes=24 << 20),
     )(*args)
+
+
+def add(a, b):
+    return (a.astype(F32) + b.astype(F32)).astype(BF16)
 
 
 def reduce_kernel(
@@ -406,9 +414,9 @@
                 sib_copy(n, axis, o, core).wait_recv()
                 q = at(axis, o)
                 if axis == "y":
-                    acc[n][q] = (w[n][core, q] + sib[n][q]).astype(BF16)
+                    acc[n][q] = add(w[n][core, q], sib[n][q])
                 else:
-                    acc[n][:, q] = (w[n][core, :, q] + sib[n][:, q]).astype(BF16)
+                    acc[n][:, q] = add(w[n][core, :, q], sib[n][:, q])
                 if o:
                     i = n * 32 + (8 if axis == "zh" else 0) + o
                     given[n].append(
@@ -465,8 +473,8 @@
 def reduced(part, wa, wb):
     vmem = pl.BlockSpec(memory_space=pltpu.VMEM)
 
-    def pair(*lead, kind=BF16):
-        return [pltpu.VMEM((*lead, 2 * SUB, BLK), kind), pltpu.VMEM((*lead, SUB, BLK), kind)]
+    def pair(*lead):
+        return [pltpu.VMEM((*lead, 2 * SUB, BLK), BF16), pltpu.VMEM((*lead, SUB, BLK), BF16)]
 
     return pl.pallas_call(
         reduce_kernel,
@@ -479,7 +487,7 @@
         out_specs=(vmem,) * 2,
         scratch_shapes=[
             pltpu.VMEM((TOK, 512), BF16),
-            *pair(8, 4, kind=F32),
+            *pair(8, 4),
             *pair(8, 4),
             *pair(8, 4),
             *pair(4, 8),

time: 60 us -> 59.8 us (level)
  no operation moved by 1% of the time
where the time goes in v4:
time: 59.8 us; the launch traced here: 58.8 us
  Pallas kernels  58.2 us (97%)
  between operations  0.66 us (1%)
    pallas_call x1, Pallas kernels, gathered(): pl.pallas_call(gather_kernel, name='gather_blocks', out_shape=(jax.ShapeD...  26.5 us
    pallas_call x1, Pallas kernels, reduced(): pl.pallas_call(reduce_kernel, name='sum_grads', out_shape=(jax.ShapeDtype...  23.6 us
    pallas_call x1, Pallas kernels, computed(): pl.pallas_call(compute_kernel, name='block_grads', out_shape=(jax.ShapeDt...  7.28 us

profile of v4, /device:TPU:1, one launch (start us, length us, event | category | flops | bytes accessed | tf_op | source)
XLA Modules:
  0.0 58.8 jit_solution(10597601700624900855)
XLA Ops:
  0.6 26.5 %gather_blocks.1 = (bf16[8,256,1024]{2,1,0:T(8,128)(2,1)S(1)}, bf16[8,128,1024]{2,1,0:T(8,128)(2,1)S(1)}, bf16[144,4096]{1,0:T(8,128)(2,1)S(1)}, bf16[144,4096]{1,0:T(8,128)(2,1)S(1)}, s32[8,128]{1,0:T(8,128)S(1)}) custom-call(bf16[1,128,128]{2,1,0:T(8,128)(2,1)} %gate.1, bf16[1,128,128]{2,1,0:T(8,128)(2,1)} %up.1, bf16[1,128,128]{2,1,0:T(8,128)(2,1)} %down.1, ...), custom_call_target="tpu_custom_call" | custom-call | tf_op jit(solution)/shard_map/gather_blocks/pallas_call | solution.py:220
  27.1 7.3 %block_grads.1 = (bf16[8,144,512]{2,1,0:T(8,128)(2,1)S(1)}, bf16[2,8,4,32,128]{4,3,2,1,0:T(8,128)(2,1)S(1)}, bf16[2,8,4,16,128]{4,3,2,1,0:T(8,128)(2,1)S(1)}) custom-call(bf16[8,256,1024]{2,1,0:T(8,128)(2,1)S(1)} %get-tuple-element.14.w, bf16[8,128,1024]{2,1,0:T(8,128)(2,1)S(1)} %get-tuple-element.15.dn, bf16[144,4096]{1,0:T(8,128)(2,1)S(1)} %get-tuple-element.16.tok, ...), custom_call_target="tpu_custom_call" | custom-call | tf_op jit(solution)/shard_map/block_grads/pallas_call | solution.py:333
  34.4 23.6 %sum_grads.1 = (bf16[7,144,512]{2,1,0:T(8,128)(2,1)S(1)}, bf16[8,48,128]{2,1,0:T(8,128)(2,1)S(1)}) custom-call(bf16[8,144,512]{2,1,0:T(8,128)(2,1)S(1)} %get-tuple-element.19.part, bf16[2,8,4,32,128]{4,3,2,1,0:T(8,128)(2,1)S(1)} %get-tuple-element.20.wa, bf16[2,8,4,16,128]{4,3,2,1,0:T(8,128)(2,1)S(1)} %get-tuple-element.21.wb), custom_call_target="tpu_custom_call" | custom-call | tf_op jit(solution)/shard_map/sum_grads/pallas_call | solution.py:479
  58.0 0.8 %write_grads.1 = (bf16[144,512]{1,0:T(8,128)(2,1)}, f32[1,128,128]{2,1,0:T(8,128)}, f32[1,128,128]{2,1,0:T(8,128)}, f32[1,128,128]{2,1,0:T(8,128)}) custom-call(bf16[8,144,512]{2,1,0:T(8,128)(2,1)S(1)} %get-tuple-element.19.part, bf16[7,144,512]{2,1,0:T(8,128)(2,1)S(1)} %get-tuple-element.22.ig_in, bf16[8,48,128]{2,1,0:T(8,128)(2,1)S(1)} %get-tuple-element.23.fin), custom_call_target="tpu_custom_call" | custom-call | tf_op jit(solution)/shard_map/write_grads/pallas_call | solution.py:527

commit v5 on v4

--- a/solution.py
+++ b/solution.py
@@ -151,9 +151,12 @@
             i = n * 16 + (8 if axis == "zh" else 0) + o
             return send(src, dst, s_sem.at[i], r_sem.at[i], {axis: at(axis, o)})
 
-        one, two, shared = {}, {}, []
+        one, early, two, shared = {}, {}, {}, []
         for first, own, buf, _, n in parts:
             one[n] = [cross(first, n, o, own, buf.at[y, z]) for o in OFF[first]]
+        for first, own, buf, _, n in parts[::-1]:
+            after = OTHER[first]
+            early[n] = [cross(after, n, o, own, buf.at[y, z]) for o in OFF[after]]
 
         prepare()
 
@@ -163,11 +166,28 @@
             shared.append(send(part, part, s_sib.at[i], r_sib.at[i], sibling()))
 
         for first, _, buf, _, n in parts[::-1]:
-            for copy in one[n]:
+            after = OTHER[first]
+            for o, copy in zip(OFF[first], one[n]):
                 copy.wait_recv()
-            held = line(buf, OTHER[first], here[OTHER[first]])
-            two[n] = [cross(OTHER[first], n, o, held, held) for o in OFF[OTHER[first]]]
-            share(OTHER[first], buf, 0, n)
+                q = at(first, -o)
+                piece = buf.at[q, z] if first == "y" else buf.at[y, q]
+                for p in OFF[after]:
+                    cross(after, n, p, piece, piece)
+            share(after, buf, 0, n)
+            two[n] = []
+            for o in OFF[after]:
+                i = n * 16 + (8 if after == "zh" else 0) + o
+                whole = line(buf, after, at(after, -o))
+                two[n].append(
+                    pltpu.make_async_remote_copy(
+                        src_ref=whole,
+                        dst_ref=whole,
+                        send_sem=s_sem.at[i],
+                        recv_sem=r_sem.at[i],
+                        device_id={after: at(after, o)},
+                        device_id_type=MESH_ID,
+                    )
+                )
         (_, _, z_buf, _, zn), (_, _, y_buf, _, yn) = parts
         arrivals = list(zip(Y_OFF, two[yn]))[::-1]
         for o, copy in arrivals[:4]:

time: 59.8 us -> 59.5 us (level); the launches traced: 58.8 us -> 59.7 us
  Pallas kernels: 58.2 us -> 59.1 us
    pallas_call x1, Pallas kernels: 23.6 us -> 24.5 us  [reduced(): pl.pallas_call(reduce_kernel, name='sum_grads', out_shape=(jax.ShapeDtype...]
    pallas_call x1, Pallas kernels: 26.5 us -> 25.6 us  [gathered(): pl.pallas_call(gather_kernel, name='gather_blocks', out_shape=(jax.ShapeD...]
    pallas_call x1, Pallas kernels: 7.28 us -> 8.07 us  [computed(): pl.pallas_call(compute_kernel, name='block_grads', out_shape=(jax.ShapeDt...]
where the time goes in v5:
time: 59.5 us; the launch traced here: 59.7 us
  Pallas kernels  59.1 us (99%)
  between operations  0.66 us (1%)
    pallas_call x1, Pallas kernels, gathered(): pl.pallas_call(gather_kernel, name='gather_blocks', out_shape=(jax.ShapeD...  25.6 us
    pallas_call x1, Pallas kernels, reduced(): pl.pallas_call(reduce_kernel, name='sum_grads', out_shape=(jax.ShapeDtype...  24.5 us
    pallas_call x1, Pallas kernels, computed(): pl.pallas_call(compute_kernel, name='block_grads', out_shape=(jax.ShapeDt...  8.07 us

profile of v5, /device:TPU:1, one launch (start us, length us, event | category | flops | bytes accessed | tf_op | source)
XLA Modules:
  0.0 59.7 jit_solution(17678417252830921385)
XLA Ops:
  0.6 25.6 %gather_blocks.1 = (bf16[8,256,1024]{2,1,0:T(8,128)(2,1)S(1)}, bf16[8,128,1024]{2,1,0:T(8,128)(2,1)S(1)}, bf16[144,4096]{1,0:T(8,128)(2,1)S(1)}, bf16[144,4096]{1,0:T(8,128)(2,1)S(1)}, s32[8,128]{1,0:T(8,128)S(1)}) custom-call(bf16[1,128,128]{2,1,0:T(8,128)(2,1)} %gate.1, bf16[1,128,128]{2,1,0:T(8,128)(2,1)} %up.1, bf16[1,128,128]{2,1,0:T(8,128)(2,1)} %down.1, ...), custom_call_target="tpu_custom_call" | custom-call | tf_op jit(solution)/shard_map/gather_blocks/pallas_call | solution.py:240
  26.3 8.1 %block_grads.1 = (bf16[8,144,512]{2,1,0:T(8,128)(2,1)S(1)}, bf16[2,8,4,32,128]{4,3,2,1,0:T(8,128)(2,1)S(1)}, bf16[2,8,4,16,128]{4,3,2,1,0:T(8,128)(2,1)S(1)}) custom-call(bf16[8,256,1024]{2,1,0:T(8,128)(2,1)S(1)} %get-tuple-element.14.w, bf16[8,128,1024]{2,1,0:T(8,128)(2,1)S(1)} %get-tuple-element.15.dn, bf16[144,4096]{1,0:T(8,128)(2,1)S(1)} %get-tuple-element.16.tok, ...), custom_call_target="tpu_custom_call" | custom-call | tf_op jit(solution)/shard_map/block_grads/pallas_call | solution.py:353
  34.3 24.5 %sum_grads.1 = (bf16[7,144,512]{2,1,0:T(8,128)(2,1)S(1)}, bf16[8,48,128]{2,1,0:T(8,128)(2,1)S(1)}) custom-call(bf16[8,144,512]{2,1,0:T(8,128)(2,1)S(1)} %get-tuple-element.19.part, bf16[2,8,4,32,128]{4,3,2,1,0:T(8,128)(2,1)S(1)} %get-tuple-element.20.wa, bf16[2,8,4,16,128]{4,3,2,1,0:T(8,128)(2,1)S(1)} %get-tuple-element.21.wb), custom_call_target="tpu_custom_call" | custom-call | tf_op jit(solution)/shard_map/sum_grads/pallas_call | solution.py:499
  58.9 0.8 %write_grads.1 = (bf16[144,512]{1,0:T(8,128)(2,1)}, f32[1,128,128]{2,1,0:T(8,128)}, f32[1,128,128]{2,1,0:T(8,128)}, f32[1,128,128]{2,1,0:T(8,128)}) custom-call(bf16[8,144,512]{2,1,0:T(8,128)(2,1)S(1)} %get-tuple-element.19.part, bf16[7,144,512]{2,1,0:T(8,128)(2,1)S(1)} %get-tuple-element.22.ig_in, bf16[8,48,128]{2,1,0:T(8,128)(2,1)S(1)} %get-tuple-element.23.fin), custom_call_target="tpu_custom_call" | custom-call | tf_op jit(solution)/shard_map/write_grads/pallas_call | solution.py:547
